TPU v7x, 256 devices: a whole 4x4x8 slice. The times are simulated.
256 devices in a mesh: wide: 16 (over z_hi, y), narrow: 16 (over z_lo, x, core).
Axes of the slice: x: 4, y: 4, z: 8 (z_hi: 4, z_lo: 2; z = z_hi * 2 + z_lo), core: 2. Of those that a mesh axis runs over, the one named last changes fastest.
Arguments:
- points: bfloat16 [65536, 768], P(('wide', 'narrow')), may hold values from -2 to 2
- centroids: bfloat16 [16384, 768], P('narrow'), may hold values from -1 to 1
Outputs:
- new_centroids: bfloat16 [16384, 768], P('narrow')
- counts: float32 [16384], P('narrow')
All inputs are finite; a program needn't handle non-finite values.
Results may differ from a plain program's by a relative error of at most 0.0036.
Values may be sent and summed in bfloat16 or wider, within the bound.
A program may use at most 128 MiB of HBM per device.

v0:
```python
import jax
import jax.numpy as jnp
from jax import lax
from jax.sharding import PartitionSpec as P


def on_device(points, centroids):
    group = lax.all_gather(points, "narrow", axis=0, tiled=True)
    logits = 60.0 * lax.dot_general(
        group, centroids, (((1,), (1,)), ((), ())), preferred_element_type=jnp.float32
    )
    local_max = jnp.max(logits, axis=1)
    row_max = lax.pmax(local_max, "narrow")
    expo = jnp.exp(logits - row_max[:, None])
    row_total = lax.psum(jnp.sum(expo, axis=1), "narrow")
    resp = (expo / row_total[:, None]).astype(jnp.bfloat16)
    sums = lax.dot_general(
        resp, group, (((0,), (0,)), ((), ())), preferred_element_type=jnp.float32
    )
    counts = jnp.sum(resp.astype(jnp.float32), axis=0)
    sums, counts = lax.psum((sums, counts), "wide")
    scale = lax.rsqrt(jnp.sum(sums * sums, axis=1, keepdims=True) + 1e-06)
    return ((sums * scale).astype(jnp.bfloat16), counts)


def solution(mesh):
    placed = (P(("wide", "narrow"), None), P("narrow", None))
    return jax.shard_map(
        on_device,
        mesh=mesh,
        in_specs=placed,
        out_specs=(P("narrow", None), P("narrow")),
        check_vma=False,
    )
```

profile of v0, /device:TPU:8, one launch (start us, length us, event | category | flops | bytes accessed | tf_op | source)
XLA Modules:
  0.0 410.1 jit_solution(14322670475185094294)
XLA Ops:
  7.2 0.0 copy-start
  7.2 0.0 all-gather.2.cloned.1.call-start
  7.2 0.7 all-gather.2.cloned.1.call-update
  7.9 0.0 all-reduce.2.cloned.1.call-start
  8.0 49.7 %all-gather.2.cloned.1.call-done = bf16[4096,768]{1,0:T(8,128)(2,1)} async-done(((bf16[256,768]{1,0:T(8,128)(2,1)}), bf16[4096,768]{1,0:T(8,128)(2,1)}) %all-gather.2.cloned.1.call-update) | async-done | bytes 6291472 | tf_op jit(solution)/shard_map/all_gather | solution.py:8
  57.7 0.0 copy-done
  57.7 12.4 %multiply_reduce_fusion = (f32[4096]{0:T(1024)S(1)}, f32[4096,1024]{0,1:T(8,128)}) fusion(bf16[4096,768]{1,0:T(8,128)(2,1)} %all-gather.2.cloned.1.call-done, bf16[1024,768]{1,0:T(8,128)(2,1)S(1)} %copy-done), kind=kOutput, calls=%fused_computation.3 | convolution fusion | flops 6450835456 | bytes 24657920 | tf_op jit(solution)/shard_map/dot_general | solution.py:9
  70.1 55.4 %pmax.7 = f32[4096]{0:T(1024)S(1)} all-reduce(f32[4096]{0:T(1024)S(1)} %get-tuple-element.4), channel_id=1, replica_groups=mesh['wide'=16,'narrow'=16] {'narrow'}, use_global_device_ids=true, to_apply=%region_1.0 | all-reduce | flops 4096 | bytes 32768 | tf_op jit(solution)/shard_map/pmax | solution.py:13
  125.5 8.5 %fusion = f32[4096]{0:T(1024)S(1)} fusion(f32[4096,1024]{0,1:T(8,128)} %get-tuple-element.5, f32[4096]{0:T(1024)S(1)} %pmax.7), kind=kLoop, calls=%fused_computation.4 | loop fusion | flops 12578816 | bytes 16809984 | tf_op jit(solution)/shard_map/reduce_sum | solution.py:15
  134.1 52.9 %psum.21 = f32[4096]{0:T(1024)S(1)} all-reduce(f32[4096]{0:T(1024)S(1)} %fusion), channel_id=1, replica_groups=mesh['wide'=16,'narrow'=16] {'narrow'}, use_global_device_ids=true, to_apply=%region_3.0 | all-reduce | flops 4096 | bytes 32768 | tf_op jit(solution)/shard_map/psum | solution.py:15
  186.9 7.8 %convert_reduce_fusion = (f32[1024]{0:T(1024)S(1)}, bf16[4096,1024]{0,1:T(8,128)(2,1)S(1)}) fusion(f32[4096]{0:T(1024)S(1)} %psum.21, f32[4096]{0:T(1024)S(1)} %pmax.7, f32[4096,1024]{0,1:T(8,128)} %get-tuple-element.5), kind=kLoop, calls=%fused_computation | loop fusion | flops 25164800 | bytes 25202688 | tf_op jit(solution)/shard_map/reduce_sum | solution.py:20
  194.8 11.1 %fusion.1 = f32[1024,768]{1,0:T(8,128)} fusion(bf16[4096,1024]{0,1:T(8,128)(2,1)S(1)} %get-tuple-element.3, bf16[4096,768]{1,0:T(8,128)(2,1)} %all-gather.2.cloned.1.call-done), kind=kOutput, calls=%fused_computation.8 | convolution fusion | flops 6442450944 | bytes 17825792 | tf_op jit(solution)/shard_map/dot_general | solution.py:17
  205.9 0.0 all-reduce.2.cloned.1.call-update
  205.9 41.6 %psum.23 = f32[1024]{0:T(1024)} all-reduce(f32[1024]{0:T(1024)S(1)} %get-tuple-element.2), channel_id=1, replica_groups=mesh['wide'=16,'narrow'=16] {'wide'}, use_global_device_ids=true, to_apply=%region_7.0 | all-reduce | flops 1024 | bytes 8192 | tf_op jit(solution)/shard_map/psum | solution.py:21
  247.5 150.3 %all-reduce.2.cloned.1.call-done = f32[1024,768]{1,0:T(8,128)} async-done(((f32[1024,768]{1,0:T(8,128)}), f32[1024,768]{1,0:T(8,128)}) %all-reduce.2.cloned.1.call-update) | async-done | bytes 3145744 | tf_op jit(solution)/shard_map/psum | solution.py:21
  397.8 2.2 multiply_reduce_fusion.1
  400.0 3.3 multiply_convert_fusion
  (1 shorter events, 0.0 us)
Async XLA Ops:
  7.2 50.5 %copy-start = (bf16[1024,768]{1,0:T(8,128)(2,1)S(1)}, bf16[1024,768]{1,0:T(8,128)(2,1)}, u32[]{:S(2)}) copy-start(bf16[1024,768]{1,0:T(8,128)(2,1)} %param.3) | copy-start | bytes 4718596
  7.2 50.5 %all-gather.2.cloned.1.call-start = ((), (), s32[]{:S(2)}) async-start(), calls=%async_computation | async-start | bytes 6684672 | tf_op jit(solution)/shard_map/all_gather | solution.py:8
  7.9 389.9 %all-reduce.2.cloned.1.call-start = ((), (), s32[]{:S(2)}) async-start(), calls=%async_computation.1 | async-start | bytes 6291456 | tf_op jit(solution)/shard_map/psum | solution.py:21
Sparse Core Ops, SparseCore 0:
  9.9 47.7 all-gather.1
  206.0 191.7 all-reduce.1
where the time goes:
time: 411 us; the launch traced here: 410 us
  waiting for transfers between devices  201 us (49%)
  blocking collectives  150 us (36%)
  matrix products  23.5 us (6%)
  other arithmetic  21.8 us (5%)
  between operations  14.1 us (3%)
    psum x1, waiting for transfers between devices, on_device(): sums, counts = lax.psum((sums, counts), 'wide')  150 us
    pmax x1, blocking collectives, on_device(): row_max = lax.pmax(local_max, 'narrow')  55.4 us
    psum x1, blocking collectives, on_device(): row_total = lax.psum(jnp.sum(expo, axis=1), 'narrow')  52.9 us
    all_gather x1, waiting for transfers between devices, on_device(): group = lax.all_gather(points, 'narrow', axis=0, tiled=True)  49.7 us
    psum x1, blocking collectives, on_device(): sums, counts = lax.psum((sums, counts), 'wide')  41.6 us
    dot_general x1, matrix products, on_device(): lax.dot_general(group, centroids, (((1,), (1,)), ((), ())), preferred_ele...  12.4 us
    dot_general x1, matrix products, on_device(): lax.dot_general(resp, group, (((0,), (0,)), ((), ())), preferred_element_...  11.1 us
    reduce_sum x1, other arithmetic, on_device(): row_total = lax.psum(jnp.sum(expo, axis=1), 'narrow')  8.53 us
  transfers between devices with their start and end apart: 2, of which 2 were waited for; matrix products, arithmetic and copies ran while one was open for 0% of the time, Pallas kernels for 0%

commit v1 on v0

v1 whole, which is shorter than its diff:
```python
import functools

import jax
import jax.numpy as jnp
from jax import lax
from jax.experimental import pallas as pl
from jax.experimental.pallas import tpu as pltpu
from jax.sharding import PartitionSpec as P

MESH = pl.DeviceIdType.MESH
F32 = jnp.float32
BF16 = jnp.bfloat16
D = 768
NS = 4
R = 128 // NS
G = 8 * R
KB = 256
RATE = 60.0 * 1.4426950408889634


def kernel(
    pts_in, cen_in, out_ref, cnt_out,
    pts, cen, e, m_tile, t_tile, s_tile, st_send, st_recv, z2_send, z2_recv,
    acc, cacc, yb, ry2, rym, zb, rz, outv, cnt, cnt_y, cnt_z,
    g_send, g_recv, loc_sem, st_ss, st_rs, z2_ss, z2_rs,
    ry_ss, ry_rs, rz_ss, rz_rs, az_ss, az_rs, ay_ss, ay_rs, c_ss, c_rs, io_sem,
):
    wide, narrow = lax.axis_index("wide"), lax.axis_index("narrow")
    h, y = wide // 4, wide % 4
    zl, x, c = narrow // 8, (narrow // 2) % 4, narrow % 2
    z = 2 * h + zl
    xm, xp, x2 = (x + 3) % 4, (x + 1) % 4, (x + 2) % 4

    def at(dx=0, dy=0, dz=0, dc=0):
        zz = (z + dz + 8) % 8
        return (
            (zz // 2) * 4 + (y + dy + 4) % 4,
            (zz % 2) * 8 + ((x + dx + 4) % 4) * 2 + (c + dc) % 2,
        )

    def send(src, dst, ss, rs, device):
        return pltpu.make_async_remote_copy(
            src_ref=src, dst_ref=dst, send_sem=ss, recv_sem=rs, device_id=device, device_id_type=MESH
        )

    mates = [(d // 2, d % 2) for d in range(1, 8)]
    cen_copy = pltpu.make_async_copy(cen_in, cen, io_sem.at[0])
    cen_copy.start()

    partners = [at(dx=a, dc=b) for a, b in mates]
    partners += [at(dz=1), at(dz=-1), at(dy=1), at(dy=2), at(dy=3), at(dz=2), at(dz=4), at(dz=6)]
    barrier = pltpu.get_barrier_semaphore()
    for device in partners:
        pl.semaphore_signal(barrier, inc=1, device_id=device, device_id_type=MESH)
    pl.semaphore_wait(barrier, len(partners))

    def own(i):
        return pts_in.at[:, pl.ds(i * R, R)]

    def gcopy(i, n):
        ss, rs = g_send.at[i, n], g_recv.at[i, n]
        if n == 0:
            return send(own(i), pts.at[i, pl.ds(0, 2), x, c], ss, rs, at(dx=1))
        if n == 1:
            return send(own(i), pts.at[i, pl.ds(0, 2), x, c], ss, rs, at(dx=-1))
        if n == 2:
            return send(pts.at[i, 0, xm, c], pts.at[i, 0, xm, c], ss, rs, at(dx=1))
        if n == 3:
            return send(pts.at[i, 1, xp, c], pts.at[i, 1, xp, c], ss, rs, at(dx=-1))
        if n == 4:
            return send(pts_in.at[0, pl.ds(i * R, R)], pts.at[i, 2, x, c], ss, rs, at(dz=1))
        if n == 5:
            return send(pts_in.at[1, pl.ds(i * R, R)], pts.at[i, 3, x, c], ss, rs, at(dz=-1))
        if n in (6, 8, 10):
            o = {6: xm, 8: xp, 10: x2}[n]
            return send(pts.at[i, 0, o, c], pts.at[i, 2, o, c], ss, rs, at(dz=1))
        if n in (7, 9, 11):
            o = {7: xm, 9: xp, 11: x2}[n]
            return send(pts.at[i, 1, o, c], pts.at[i, 3, o, c], ss, rs, at(dz=-1))
        if n == 12:
            half = pts.at[i, pl.ds(0, 2), :, c]
        else:
            half = pts.at[i, n - 11, :, c]
        return send(half, half, ss, rs, at(dc=1))

    def local(i):
        return pltpu.make_async_copy(own(i), pts.at[i, pl.ds(0, 2), x, c], loc_sem.at[i])

    def start(i, *ns):
        for n in ns:
            gcopy(i, n).start()

    def arrived(i, *ns):
        for n in ns:
            gcopy(i, n).wait_recv()

    def ev0(i):
        start(i, 0, 1, 4, 5)
        local(i).start()

    def ev1(i):
        arrived(i, 0, 1)
        start(i, 2, 3, 6, 7, 8, 9)

        @pl.when(i + 1 < NS)
        def _():
            ev0(i + 1)

    def ev2(i):
        arrived(i, 2, 3)
        start(i, 10, 11)
        local(i).wait()
        start(i, 12)

    def ev3(i):
        arrived(i, 4, 6, 8, 10)
        start(i, 13)
        arrived(i, 5, 7, 9, 11)
        start(i, 14)

    def mm1(i, g):
        p = pts[i, g].reshape(G, D)
        for k in range(4):
            l = lax.dot_general(
                cen[k * KB : (k + 1) * KB, :], p, (((1,), (1,)), ((), ())), preferred_element_type=F32
            )
            m = jnp.max(l, axis=0, keepdims=True)
            v = jnp.exp2((l - m) * RATE)
            e[i, g, k * KB : (k + 1) * KB, :] = v
            t = jnp.sum(v, axis=0, keepdims=True)
            for j in range(2):
                m_tile[i, k, 2 * g + j : 2 * g + j + 1, :] = m[:, j * 128 : (j + 1) * 128]
                t_tile[i, k, 2 * g + j : 2 * g + j + 1, :] = t[:, j * 128 : (j + 1) * 128]

    def st_copy(i, d):
        a, b = mates[d]
        return send(st_send.at[i], st_recv.at[i, d], st_ss.at[i, d], st_rs.at[i, d], at(dx=a, dc=b))

    def z2_copy(i, d):
        return send(z2_send.at[i], z2_recv.at[i, d], z2_ss.at[i, d], z2_rs.at[i, d], at(dz=1 - 2 * d))

    def merge(parts):
        m = functools.reduce(jnp.maximum, [a for a, _ in parts])
        return m, sum(t * jnp.exp2((a - m) * RATE) for a, t in parts)

    def st1(i):
        m, t = merge([(m_tile[i, k], t_tile[i, k]) for k in range(4)])
        st_send[i, 0] = m
        st_send[i, 1] = t
        for d in range(7):
            st_copy(i, d).start()

    def st2(i):
        for d in range(7):
            st_copy(i, d).wait_recv()
        parts = [(st_send[i, 0], st_send[i, 1])]
        parts += [(st_recv[i, d, 0], st_recv[i, d, 1]) for d in range(7)]
        m, t = merge(parts)
        z2_send[i, 0] = m
        z2_send[i, 1] = t
        for d in range(2):
            z2_copy(i, d).start()

    def st3(i):
        for d in range(2):
            z2_copy(i, d).wait_recv()
        row = lax.broadcasted_iota(jnp.int32, (8, 128), 0)
        above = (row < 2) | (row >= 6)

        def other(n):
            lo, hi = z2_recv[i, 0, n], z2_recv[i, 1, n]
            turn = lambda a: jnp.concatenate([a[4:], a[:4]], axis=0)
            return jnp.where(above, turn(hi), turn(lo))

        m, t = merge([(z2_send[i, 0], z2_send[i, 1]), (other(0), other(1))])
        inv = 1.0 / t
        for k in range(4):
            s_tile[i, k] = jnp.exp2((m_tile[i, k] - m) * RATE) * inv

    ev0(0)
    ev1(0)
    ev2(0)
    cen_copy.wait()
    arrived(0, 12)

    def step(i, carry):
        @pl.when(i < NS)
        def _():
            mm1(i, 0)

        @pl.when(i > 0)
        def _():
            ev3(i - 1)

        @pl.when(i + 1 < NS)
        def _():
            ev1(i + 1)

        @pl.when(i < NS)
        def _():
            mm1(i, 1)

        @pl.when(i > 0)
        def _():
            arrived(i - 1, 13, 14)
            mm1(i - 1, 2)

        @pl.when(i + 1 < NS)
        def _():
            ev2(i + 1)

        @pl.when(i > 0)
        def _():
            mm1(i - 1, 3)
            st1(i - 1)

        @pl.when(i > 1)
        def _():
            st2(i - 2)

        @pl.when(i + 1 < NS)
        def _():
            arrived(i + 1, 12)

        return carry

    lax.fori_loop(0, NS + 1, step, 0)

    deltas = (2, 1, 3, 0)

    def mm2(n, lo, hi):
        b = (h + deltas[n]) % 4
        r0 = pl.multiple_of(b * KB, KB)

        def part(i, carry):
            cs = jnp.zeros((KB, 128), F32)
            resp = []
            for g in range(4):
                for j in range(2):
                    v = e[i, g, pl.ds(r0, KB), j * 128 : (j + 1) * 128] * s_tile[i, b, 2 * g + j : 2 * g + j + 1, :]
                    cs = cs + v
                    resp.append(v.astype(BF16))
            cacc[pl.ds(r0, KB), :] += cs
            acc[n] += jnp.dot(
                jnp.concatenate(resp, axis=1), pts[i].reshape(4 * G, D), preferred_element_type=F32
            )
            return carry

        lax.fori_loop(lo, hi, part, 0)

    ym, yp, y2 = (y + 3) % 4, (y + 1) % 4, (y + 2) % 4

    def half(ref, owner, side):
        return ref.at[pl.ds(pl.multiple_of(owner * 64 + side * 32, 32), 32)]

    def ycopy(n, q):
        up, kind = q % 2 == 0, q // 2
        ss, rs = ry_ss.at[n, q], ry_rs.at[n, q]
        to = at(dy=1 if up else -1)
        near = yp if up else ym
        side = 0 if up else 1
        if kind == 0:
            return send(half(yb.at[n], y2, side), ry2.at[n, side], ss, rs, to)
        if kind == 1:
            return send(half(yb.at[n], near, 1 - side), rym.at[n, side, pl.ds((1 - side) * 32, 32)], ss, rs, to)
        return send(half(yb.at[n], near, side), rym.at[n, side, pl.ds(side * 32, 32)], ss, rs, to)

    def rs_a(n):
        yb[n] = acc[n].astype(BF16)
        for q in range(4):
            ycopy(n, q).start()

    def rs_b(n):
        for side, near in ((0, yp), (1, ym)):
            ycopy(n, side).wait_recv()
            rows = pl.ds(pl.multiple_of(near * 64 + side * 32, 32), 32)
            yb[n, rows] = (acc[n, rows] + ry2[n, side].astype(F32)).astype(BF16)
            ycopy(n, 4 + side).start()

    def zcopy(n):
        return send(zb.at[n], rz.at[n], rz_ss.at[n], rz_rs.at[n], at(dz=2 * deltas[n]))

    def rs_c(n):
        for q in range(2, 6):
            ycopy(n, q).wait_recv()
        total = acc[n, pl.ds(pl.multiple_of(y * 64, 64), 64)]
        total = total + rym[n, 0].astype(F32) + rym[n, 1].astype(F32)
        if n < 3:
            zb[n] = total.astype(BF16)
            zcopy(n).start()
        return total

    acc[...] = jnp.zeros_like(acc)
    cacc[...] = jnp.zeros_like(cacc)
    for i in range(NS - 1):
        st3(i)
    st2(NS - 1)
    mm2(0, 0, NS - 1)
    st3(NS - 1)
    mm2(0, NS - 1, NS)
    rs_a(0)
    mm2(1, 0, NS)
    rs_a(1)
    rs_b(0)
    mm2(2, 0, NS)
    rs_a(2)
    rs_b(1)
    rs_c(0)
    mm2(3, 0, NS)
    rs_a(3)
    rs_b(2)
    rs_c(1)

    rest, wide_cnt = cacc[...], jnp.zeros((8, 1024), F32)
    ones = jnp.ones((8, 128), BF16)
    for _ in range(3):
        term = rest.astype(BF16)
        wide_cnt += lax.dot_general(ones, term, (((1,), (1,)), ((), ())), preferred_element_type=F32)
        rest = rest - term.astype(F32)
    row = lax.broadcasted_iota(jnp.int32, (8, 128), 0)
    dense = jnp.zeros((8, 128), F32)
    for r in range(8):
        dense = jnp.where(row == r, wide_cnt[:, r * 128 : (r + 1) * 128], dense)
    cnt[0] = dense

    def ccopy(n):
        d = n % 3 + 1
        if n < 3:
            return send(cnt.at[0], cnt_y.at[d - 1], c_ss.at[n], c_rs.at[n], at(dy=d))
        return send(cnt.at[1], cnt_z.at[d - 1], c_ss.at[n], c_rs.at[n], at(dz=2 * d))

    for n in range(3):
        ccopy(n).start()
    rs_b(3)
    rs_c(2)
    total = rs_c(3)
    for n in range(3):
        ccopy(n).wait_recv()
    cnt[1] = cnt[0] + cnt_y[0] + cnt_y[1] + cnt_y[2]
    for n in range(3, 6):
        ccopy(n).start()
    for n in range(3):
        zcopy(n).wait_recv()
        total = total + rz[n].astype(F32)

    scale = lax.rsqrt(jnp.sum(total * total, axis=1, keepdims=True) + 1e-06)
    outv[h, y] = (total * scale).astype(BF16)

    def azcopy(d):
        return send(outv.at[h, y], outv.at[h, y], az_ss.at[d], az_rs.at[d], at(dz=2 * d))

    def aycopy(b, n, q):
        up, forward = q % 2 == 0, q >= 2
        to, ss, rs = at(dy=1 if up else -1), ay_ss.at[n, q], ay_rs.at[n, q]
        if not forward:
            return send(outv.at[b, y], outv.at[b, y], ss, rs, to)
        block = outv.at[b, ym if up else yp, pl.ds(0 if up else 32, 32)]
        return send(block, block, ss, rs, to)

    order = (0, 1, 3, 2)
    for d in (1, 3, 2):
        azcopy(d).start()

    def ag_a(n):
        d = order[n]
        if d:
            azcopy(d).wait_recv()
        for q in range(2):
            aycopy((h - d + 4) % 4, n, q).start()

    def ag_b(n):
        b = (h - order[n] + 4) % 4
        for q in range(2):
            aycopy(b, n, q).wait_recv()
            aycopy(b, n, 2 + q).start()

    def writeback(n):
        b = (h - order[n] + 4) % 4
        return pltpu.make_async_copy(outv.at[b], out_ref.at[b], io_sem.at[1 + n])

    def ag_c(n):
        b = (h - order[n] + 4) % 4
        for q in range(2, 4):
            aycopy(b, n, q).wait_recv()
        writeback(n).start()

    ag_a(0)
    ag_a(1)
    ag_b(0)
    ag_a(2)
    ag_b(1)
    ag_c(0)
    ag_a(3)
    ag_b(2)
    ag_c(1)
    ag_b(3)
    ag_c(2)
    for n in range(3, 6):
        ccopy(n).wait_recv()
    cnt_out[...] = cnt[1] + cnt_z[0] + cnt_z[1] + cnt_z[2]
    ag_c(3)

    def sent(i, carry):
        for n in range(15):
            gcopy(i, n).wait_send()
        for d in range(7):
            st_copy(i, d).wait_send()
        for d in range(2):
            z2_copy(i, d).wait_send()
        return carry

    lax.fori_loop(0, NS, sent, 0)
    for n in range(4):
        for q in range(6):
            ycopy(n, q).wait_send()
        b = (h - order[n] + 4) % 4
        for q in range(4):
            aycopy(b, n, q).wait_send()
    for n in range(3):
        zcopy(n).wait_send()
        azcopy(n + 1).wait_send()
    for n in range(6):
        ccopy(n).wait_send()
    for n in range(4):
        writeback(n).wait()


def on_device(points, centroids):
    dma = pltpu.SemaphoreType.DMA
    out, counts = pl.pallas_call(
        kernel,
        out_shape=(
            jax.ShapeDtypeStruct((4, 4, 64, D), BF16),
            jax.ShapeDtypeStruct((8, 128), F32),
        ),
        in_specs=[pl.BlockSpec(memory_space=pl.ANY)] * 2,
        out_specs=(
            pl.BlockSpec(memory_space=pl.ANY),
            pl.BlockSpec(memory_space=pltpu.VMEM),
        ),
        scratch_shapes=[
            pltpu.VMEM((NS, 4, 4, 2, R, D), BF16),
            pltpu.VMEM((1024, D), BF16),
            pltpu.VMEM((NS, 4, 1024, G), F32),
            pltpu.VMEM((NS, 4, 8, 128), F32),
            pltpu.VMEM((NS, 4, 8, 128), F32),
            pltpu.VMEM((NS, 4, 8, 128), F32),
            pltpu.VMEM((NS, 2, 8, 128), F32),
            pltpu.VMEM((NS, 7, 2, 8, 128), F32),
            pltpu.VMEM((NS, 2, 8, 128), F32),
            pltpu.VMEM((NS, 2, 2, 8, 128), F32),
            pltpu.VMEM((4, KB, D), F32),
            pltpu.VMEM((1024, 128), F32),
            pltpu.VMEM((4, KB, D), BF16),
            pltpu.VMEM((4, 2, 32, D), BF16),
            pltpu.VMEM((4, 2, 64, D), BF16),
            pltpu.VMEM((3, 64, D), BF16),
            pltpu.VMEM((3, 64, D), BF16),
            pltpu.VMEM((4, 4, 64, D), BF16),
            pltpu.VMEM((2, 8, 128), F32),
            pltpu.VMEM((3, 8, 128), F32),
            pltpu.VMEM((3, 8, 128), F32),
            dma((NS, 15)), dma((NS, 15)), dma((NS,)),
            dma((NS, 7)), dma((NS, 7)), dma((NS, 2)), dma((NS, 2)),
            dma((4, 6)), dma((4, 6)), dma((3,)), dma((3,)),
            dma((4,)), dma((4,)), dma((4, 4)), dma((4, 4)),
            dma((6,)), dma((6,)), dma((5,)),
        ],
        compiler_params=pltpu.CompilerParams(
            collective_id=0, has_side_effects=True, vmem_limit_bytes=56 << 20
        ),
        cost_estimate=pl.CostEstimate(
            flops=4 * 4096 * 1024 * D, bytes_accessed=4 << 20, transcendentals=4096 * 1024
        ),
    )(points.reshape(2, 128, D), centroids)
    return out.reshape(1024, D), counts.reshape(1024)


def solution(mesh):
    placed = (P(("wide", "narrow"), None), P("narrow", None))
    return jax.shard_map(
        on_device,
        mesh=mesh,
        in_specs=placed,
        out_specs=(P("narrow", None), P("narrow")),
        check_vma=False,
    )
```

time: 411 us -> 101 us (0.25)
  waiting for transfers between devices: 201 us -> 0 us
  blocking collectives: 150 us -> 0 us
  Pallas kernels: 0 us -> 95.9 us
  matrix products: 23.5 us -> 0 us
  other arithmetic: 21.8 us -> 0 us
  between operations: 14.1 us -> 0.65 us
    psum x1 -> x0, waiting for transfers between devices: 150 us -> none  [on_device(): sums, counts = lax.psum((sums, counts), 'wide')]
    pallas_call x0 -> x1, Pallas kernels: none -> 95.9 us  [on_device(): pl.pallas_call(kernel, out_shape=(jax.ShapeDtypeStruct((4, 4, 64, D), BF1...]
    psum x2 -> x0, blocking collectives: 94.5 us -> none  [the longest x1 52.9 us: on_device(): row_total = lax.psum(jnp.sum(expo, axis=1), 'narrow')]
    pmax x1 -> x0, blocking collectives: 55.4 us -> none  [on_device(): row_max = lax.pmax(local_max, 'narrow')]
    all_gather x1 -> x0, waiting for transfers between devices: 49.7 us -> none  [on_device(): group = lax.all_gather(points, 'narrow', axis=0, tiled=True)]
    dot_general x2 -> x0, matrix products: 23.5 us -> none  [the longest x1 12.4 us: on_device(): lax.dot_general(group, centroids, (((1,), (1,)), ((), ())), preferred_ele...]
    reduce_sum x3 -> x0, other arithmetic: 18.5 us -> none  [the longest x1 8.53 us: on_device(): row_total = lax.psum(jnp.sum(expo, axis=1), 'narrow')]
  transfers between devices with their start and end apart: 2 -> 0, of which waited for: 2 -> 0; matrix products, arithmetic and copies ran while one was open for 0% -> 0% of each run, Pallas kernels for 0% -> 0%
where the time goes in v1:
time: 101 us; the launch traced here: 99.8 us
  Pallas kernels  95.9 us (95%)
  local copies, waits for them, and re-layouts  3.25 us (3%)
    pallas_call x1, Pallas kernels, on_device(): pl.pallas_call(kernel, out_shape=(jax.ShapeDtypeStruct((4, 4, 64, D), BF1...  95.9 us
    unnamed x4, local copies, waits for them, and re-layouts  3.25 us

profile of v1, /device:TPU:8, one launch (start us, length us, event | category | flops | bytes accessed | tf_op | source)
XLA Modules:
  0.0 99.8 jit_solution(18247387645051935764)
XLA Ops:
  0.6 95.9 %shard_map.41 = (bf16[4,4,64,768]{3,2,1,0:T(8,128)(2,1)}, f32[8,128]{1,0:T(8,128)}) custom-call(bf16[2,128,768]{2,1,0:T(8,128)(2,1)} %bitcast.5, bf16[1024,768]{1,0:T(8,128)(2,1)} %cen_in.1), custom_call_target="tpu_custom_call" | custom-call | flops 12884901888 | bytes 4194304 | tf_op jit(solution)/shard_map/pallas_call | solution.py:430
  96.5 0.0 copy-start
  96.5 2.7 %copy.6 = bf16[1024,768]{1,0:T(8,128)(2,1)} copy(bf16[1024,768]{1,0:T(8,128)(2,1)} %bitcast.3) | data formatting | bytes 3145728
  99.2 0.0 copy-done
  99.2 0.6 copy.7
Async XLA Ops:
  96.5 2.7 %copy-start = (f32[8,128]{1,0:T(8,128)S(1)}, f32[8,128]{1,0:T(8,128)}, u32[]{:S(2)}) copy-start(f32[8,128]{1,0:T(8,128)} %get-tuple-element.5) | copy-start | bytes 12292

commit v2 on v1

v2 whole, which is shorter than its diff:
```python
import functools

import jax
import jax.numpy as jnp
from jax import lax
from jax.experimental import pallas as pl
from jax.experimental.pallas import tpu as pltpu
from jax.sharding import PartitionSpec as P

MESH = pl.DeviceIdType.MESH
F32 = jnp.float32
BF16 = jnp.bfloat16
D = 768
NS = 4
R = 128 // NS
G = 8 * R
KB = 256
RATE = 60.0 * 1.4426950408889634


def kernel(
    pts_in, cen_in, out_ref, cnt_out,
    pts, cen, e, m_tile, t_tile, s_tile, st_send, st_recv, z2_send, z2_recv,
    acc, cacc, yb, ry2, rym, zt, zb, rz, outv, cnt, cnt_y, cnt_z,
    g_send, g_recv, loc_sem, st_ss, st_rs, z2_ss, z2_rs,
    y2_ss, y2_rs, ym_ss, ym_rs, rz_ss, rz_rs, az_ss, az_rs, ay_ss, ay_rs, c_ss, c_rs, io_sem,
):
    wide, narrow = lax.axis_index("wide"), lax.axis_index("narrow")
    h, y = wide // 4, wide % 4
    zl, x, c = narrow // 8, (narrow // 2) % 4, narrow % 2
    z = 2 * h + zl
    xm, xp, x2 = (x + 3) % 4, (x + 1) % 4, (x + 2) % 4
    ym, yp, y2 = (y + 3) % 4, (y + 1) % 4, (y + 2) % 4

    def at(dx=0, dy=0, dz=0, dc=0):
        zz = (z + dz + 8) % 8
        return (
            (zz // 2) * 4 + (y + dy + 4) % 4,
            (zz % 2) * 8 + ((x + dx + 4) % 4) * 2 + (c + dc) % 2,
        )

    def send(src, dst, ss, rs, device):
        return pltpu.make_async_remote_copy(
            src_ref=src, dst_ref=dst, send_sem=ss, recv_sem=rs, device_id=device, device_id_type=MESH
        )

    def wait(ref, sem):
        send(ref, ref, sem, sem, at(dc=1)).wait_recv()

    mates = [(d // 2, d % 2) for d in range(1, 8)]
    cen_copy = pltpu.make_async_copy(cen_in, cen, io_sem.at[0])
    cen_copy.start()

    partners = [at(dx=a, dc=b) for a, b in mates]
    partners += [at(dz=1), at(dz=-1), at(dy=1), at(dy=2), at(dy=3), at(dz=2), at(dz=4), at(dz=6)]
    barrier = pltpu.get_barrier_semaphore()
    for device in partners:
        pl.semaphore_signal(barrier, inc=1, device_id=device, device_id_type=MESH)
    acc[...] = jnp.zeros_like(acc)
    cacc[...] = jnp.zeros_like(cacc)
    pl.semaphore_wait(barrier, len(partners))

    def own(i):
        return pts_in.at[:, pl.ds(i * R, R)]

    def gcopy(i, n):
        q = n if n < 4 else n - 6 if n >= 12 else 4 + n % 2
        ss, rs = g_send.at[q], g_recv.at[i, q]
        if n == 0:
            return send(own(i), pts.at[i, pl.ds(0, 2), x, c], ss, rs, at(dx=1))
        if n == 1:
            return send(own(i), pts.at[i, pl.ds(0, 2), x, c], ss, rs, at(dx=-1))
        if n == 2:
            return send(pts.at[i, 0, xm, c], pts.at[i, 0, xm, c], ss, rs, at(dx=1))
        if n == 3:
            return send(pts.at[i, 1, xp, c], pts.at[i, 1, xp, c], ss, rs, at(dx=-1))
        if n == 4:
            return send(pts_in.at[0, pl.ds(i * R, R)], pts.at[i, 2, x, c], ss, rs, at(dz=1))
        if n == 5:
            return send(pts_in.at[1, pl.ds(i * R, R)], pts.at[i, 3, x, c], ss, rs, at(dz=-1))
        if n in (6, 8, 10):
            o = {6: xm, 8: xp, 10: x2}[n]
            return send(pts.at[i, 0, o, c], pts.at[i, 2, o, c], ss, rs, at(dz=1))
        if n in (7, 9, 11):
            o = {7: xm, 9: xp, 11: x2}[n]
            return send(pts.at[i, 1, o, c], pts.at[i, 3, o, c], ss, rs, at(dz=-1))
        if n == 12:
            half = pts.at[i, pl.ds(0, 2), :, c]
        else:
            half = pts.at[i, n - 11, :, c]
        return send(half, half, ss, rs, at(dc=1))

    def local(i):
        return pltpu.make_async_copy(own(i), pts.at[i, pl.ds(0, 2), x, c], loc_sem.at[i])

    def start(i, *ns):
        for n in ns:
            gcopy(i, n).start()

    def arrived(i, *ns):
        for n in ns:
            gcopy(i, n).wait_recv()

    def ev0(i):
        start(i, 0, 1, 4, 5)
        local(i).start()

    def ev1(i):
        arrived(i, 0, 1)
        start(i, 2, 3, 6, 7, 8, 9)

        @pl.when(i + 2 < NS)
        def _():
            ev0(i + 2)

    def ev2(i):
        arrived(i, 2, 3)
        start(i, 10, 11)
        local(i).wait()
        start(i, 12)

    def ev3(i):
        for n in (0, 1):
            wait(pts.at[i, 2 + n, :, c], g_recv.at[i, 4 + n])
            start(i, 13 + n)

    def mm1(i, g):
        p = pts[i, g].reshape(G, D)
        for k in range(4):
            l = lax.dot_general(
                cen[k * KB : (k + 1) * KB, :], p, (((1,), (1,)), ((), ())), preferred_element_type=F32
            )
            m = jnp.max(l, axis=0, keepdims=True)
            v = jnp.exp2((l - m) * RATE)
            e[i, g, k * KB : (k + 1) * KB, :] = v
            t = jnp.sum(v, axis=0, keepdims=True)
            for j in range(2):
                m_tile[i, k, 2 * g + j : 2 * g + j + 1, :] = m[:, j * 128 : (j + 1) * 128]
                t_tile[i, k, 2 * g + j : 2 * g + j + 1, :] = t[:, j * 128 : (j + 1) * 128]

    def st_copy(i, d):
        a, b = mates[d]
        return send(st_send.at[i], st_recv.at[i, d], st_ss.at[0], st_rs.at[i], at(dx=a, dc=b))

    def z2_copy(i, d):
        return send(z2_send.at[i], z2_recv.at[i, d], z2_ss.at[0], z2_rs.at[i], at(dz=1 - 2 * d))

    def merge(parts):
        m = functools.reduce(jnp.maximum, [a for a, _ in parts])
        return m, sum(t * jnp.exp2((a - m) * RATE) for a, t in parts)

    def st1(i):
        m, t = merge([(m_tile[i, k], t_tile[i, k]) for k in range(4)])
        st_send[i, 0] = m
        st_send[i, 1] = t
        for d in range(7):
            st_copy(i, d).start()

    def st2(i):
        wait(st_recv.at[i], st_rs.at[i])
        parts = [(st_send[i, 0], st_send[i, 1])]
        parts += [(st_recv[i, d, 0], st_recv[i, d, 1]) for d in range(7)]
        m, t = merge(parts)
        z2_send[i, 0] = m
        z2_send[i, 1] = t
        for d in range(2):
            z2_copy(i, d).start()

    def st3(i):
        wait(z2_recv.at[i], z2_rs.at[i])
        row = lax.broadcasted_iota(jnp.int32, (8, 128), 0)
        above = (row < 2) | (row >= 6)

        def other(n):
            lo, hi = z2_recv[i, 0, n], z2_recv[i, 1, n]
            turn = lambda a: jnp.concatenate([a[4:], a[:4]], axis=0)
            return jnp.where(above, turn(hi), turn(lo))

        m, t = merge([(z2_send[i, 0], z2_send[i, 1]), (other(0), other(1))])
        inv = 1.0 / t
        for k in range(4):
            s_tile[i, k] = jnp.exp2((m_tile[i, k] - m) * RATE) * inv

    ev0(0)
    ev0(1)
    ev1(0)
    ev2(0)
    ev1(1)
    cen_copy.wait()
    arrived(0, 12)

    def step(i, carry):
        @pl.when(i < NS)
        def _():
            mm1(i, 0)

        @pl.when(i + 1 < NS)
        def _():
            ev2(i + 1)

        @pl.when(i < NS)
        def _():
            mm1(i, 1)

        @pl.when(i + 2 < NS)
        def _():
            ev1(i + 2)

        @pl.when(i > 1)
        def _():
            st2(i - 2)

        @pl.when(i > 0)
        def _():
            arrived(i - 1, 13, 14)
            mm1(i - 1, 2)
            mm1(i - 1, 3)
            st1(i - 1)

        @pl.when(i < NS)
        def _():
            ev3(i)

        @pl.when(i > 2)
        def _():
            st3(i - 3)

        @pl.when(i + 1 < NS)
        def _():
            arrived(i + 1, 12)

        return carry

    lax.fori_loop(0, NS + 1, step, 0)

    def mm2(n, lo, hi):
        def part(i, carry):
            cs = jnp.zeros((KB, 128), F32)
            resp = []
            for g in range(4):
                for j in range(2):
                    v = e[i, g, n * KB : (n + 1) * KB, j * 128 : (j + 1) * 128]
                    v = v * s_tile[i, n, 2 * g + j : 2 * g + j + 1, :]
                    cs = cs + v
                    resp.append(v.astype(BF16))
            cacc[n * KB : (n + 1) * KB, :] += cs
            acc[n] += jnp.dot(
                jnp.concatenate(resp, axis=1), pts[i].reshape(4 * G, D), preferred_element_type=F32
            ).reshape(4, 64, D)
            return carry

        lax.fori_loop(lo, hi, part, 0)

    def cols(side):
        return pl.ds(side * (D // 2), D // 2)

    def ycopy(n, kind, side):
        to, near = at(dy=1 - 2 * side), (yp, ym)[side]
        if kind == 0:
            return send(yb.at[n, y2, :, cols(side)], ry2.at[n, side], y2_ss.at[0], y2_rs.at[n, side], to)
        part = cols(1 - side if kind == 1 else side)
        return send(yb.at[n, near, :, part], rym.at[n, side, :, part], ym_ss.at[0], ym_rs.at[n], to)

    def rs_a(n):
        yb[n] = acc[n].astype(BF16)
        for kind in range(2):
            for side in range(2):
                ycopy(n, kind, side).start()

    def rs_b(n):
        for side, near in ((0, yp), (1, ym)):
            ycopy(n, 0, side).wait_recv()
            part = cols(side)
            yb[n, near, :, part] = (acc[n, near, :, part] + ry2[n, side].astype(F32)).astype(BF16)
            ycopy(n, 2, side).start()

    def zcopy(n, d):
        return send(zb.at[n, (h + d) % 4], rz.at[n, d - 1], rz_ss.at[0], rz_rs.at[n], at(dz=2 * d))

    def rs_c(n):
        wait(rym.at[n], ym_rs.at[n])
        total = acc[n, y] + rym[n, 0].astype(F32) + rym[n, 1].astype(F32)
        zt[n] = total.reshape(4, 16, D)
        zb[n] = total.astype(BF16).reshape(4, 16, D)
        for d in (2, 1, 3):
            zcopy(n, d).start()

    def azcopy(n, d):
        return send(outv.at[n, y, h], outv.at[n, y, h], az_ss.at[0], az_rs.at[n], at(dz=2 * d))

    def aycopy(n, q):
        side = q % 2
        to, ss, rs = at(dy=1 - 2 * side), ay_ss.at[q // 2], ay_rs.at[n, q]
        block = outv.at[n, y] if q < 2 else outv.at[n, (ym, yp)[side], :, :, cols(side)]
        return send(block, block, ss, rs, to)

    def writeback(n):
        return pltpu.make_async_copy(outv.at[n], out_ref.at[n], io_sem.at[1 + n])

    def ag_f(n):
        wait(rz.at[n], rz_rs.at[n])
        total = zt[n, h]
        for d in range(3):
            total = total + rz[n, d].astype(F32)
        scale = lax.rsqrt(jnp.sum(total * total, axis=1, keepdims=True) + 1e-06)
        outv[n, y, h] = (total * scale).astype(BF16)
        for d in (2, 1, 3):
            azcopy(n, d).start()

    def ag_g(n):
        wait(rz.at[n], az_rs.at[n])
        for q in range(2):
            aycopy(n, q).start()

    def ag_h(n):
        for q in range(2):
            aycopy(n, q).wait_recv()
            aycopy(n, 2 + q).start()

    def ag_i(n):
        for q in range(2, 4):
            aycopy(n, q).wait_recv()
        writeback(n).start()

    def ccopy(n):
        d = n % 3 + 1
        if n < 3:
            return send(cnt.at[0], cnt_y.at[d - 1], c_ss.at[0], c_rs.at[0], at(dy=d))
        return send(cnt.at[1], cnt_z.at[d - 1], c_ss.at[1], c_rs.at[1], at(dz=2 * d))

    def cnt_a():
        rest, lanes = cacc[...], jnp.zeros((8, 1024), F32)
        ones = jnp.ones((8, 128), BF16)
        for _ in range(3):
            term = rest.astype(BF16)
            lanes += lax.dot_general(ones, term, (((1,), (1,)), ((), ())), preferred_element_type=F32)
            rest = rest - term.astype(F32)
        row = lax.broadcasted_iota(jnp.int32, (8, 128), 0)
        dense = jnp.zeros((8, 128), F32)
        for r in range(8):
            dense = jnp.where(row == r, lanes[:, r * 128 : (r + 1) * 128], dense)
        cnt[0] = dense
        for n in range(3):
            ccopy(n).start()

    def cnt_b():
        wait(cnt_y, c_rs.at[0])
        cnt[1] = cnt[0] + cnt_y[0] + cnt_y[1] + cnt_y[2]
        for n in range(3, 6):
            ccopy(n).start()

    def cnt_c():
        wait(cnt_z, c_rs.at[1])
        cnt_out[...] = cnt[1] + cnt_z[0] + cnt_z[1] + cnt_z[2]

    mm2(0, 0, NS - 2)
    st3(NS - 2)
    st2(NS - 1)
    mm2(0, NS - 2, NS - 1)
    st3(NS - 1)
    mm2(0, NS - 1, NS)
    rs_a(0)
    mm2(1, 0, NS)
    rs_a(1)
    rs_b(0)
    mm2(2, 0, NS)
    rs_a(2)
    rs_b(1)
    rs_c(0)
    mm2(3, 0, NS)
    rs_a(3)
    rs_b(2)
    rs_c(1)
    ag_f(0)
    rs_b(3)
    rs_c(2)
    cnt_a()
    ag_f(1)
    rs_c(3)
    ag_g(0)
    ag_f(2)
    cnt_b()
    ag_h(0)
    ag_g(1)
    ag_f(3)
    ag_h(1)
    ag_i(0)
    ag_g(2)
    ag_h(2)
    ag_i(1)
    ag_g(3)
    cnt_c()
    ag_h(3)
    ag_i(2)
    ag_i(3)

    for n in range(2):
        wait(pts_in, g_send.at[n])
        wait(pts.at[:, 0, 0, 0], g_send.at[2 + n])
        wait(pts.at[:, 2 + n, :, c], g_send.at[4 + n])
        wait(pts.at[:, 2 + n, :, c], g_send.at[7 + n])
    wait(pts.at[:, pl.ds(0, 2), :, c], g_send.at[6])
    wait(st_recv, st_ss.at[0])
    wait(z2_recv, z2_ss.at[0])
    wait(ry2, y2_ss.at[0])
    wait(rym, ym_ss.at[0])
    wait(rz, rz_ss.at[0])
    wait(rz, az_ss.at[0])
    wait(outv.at[pl.ds(0, 2)], ay_ss.at[0])
    wait(outv.at[0], ay_ss.at[1])
    wait(cnt_y, c_ss.at[0])
    wait(cnt_z, c_ss.at[1])
    for n in range(4):
        writeback(n).wait()


def on_device(points, centroids):
    dma = pltpu.SemaphoreType.DMA
    out, counts = pl.pallas_call(
        kernel,
        out_shape=(
            jax.ShapeDtypeStruct((4, 4, 4, 16, D), BF16),
            jax.ShapeDtypeStruct((8, 128), F32),
        ),
        in_specs=[pl.BlockSpec(memory_space=pl.ANY)] * 2,
        out_specs=(
            pl.BlockSpec(memory_space=pl.ANY),
            pl.BlockSpec(memory_space=pltpu.VMEM),
        ),
        scratch_shapes=[
            pltpu.VMEM((NS, 4, 4, 2, R, D), BF16),
            pltpu.VMEM((1024, D), BF16),
            pltpu.VMEM((NS, 4, 1024, G), F32),
            pltpu.VMEM((NS, 4, 8, 128), F32),
            pltpu.VMEM((NS, 4, 8, 128), F32),
            pltpu.VMEM((NS, 4, 8, 128), F32),
            pltpu.VMEM((NS, 2, 8, 128), F32),
            pltpu.VMEM((NS, 7, 2, 8, 128), F32),
            pltpu.VMEM((NS, 2, 8, 128), F32),
            pltpu.VMEM((NS, 2, 2, 8, 128), F32),
            pltpu.VMEM((4, 4, 64, D), F32),
            pltpu.VMEM((1024, 128), F32),
            pltpu.VMEM((4, 4, 64, D), BF16),
            pltpu.VMEM((4, 2, 64, D // 2), BF16),
            pltpu.VMEM((4, 2, 64, D), BF16),
            pltpu.VMEM((4, 4, 16, D), F32),
            pltpu.VMEM((4, 4, 16, D), BF16),
            pltpu.VMEM((4, 3, 16, D), BF16),
            pltpu.VMEM((4, 4, 4, 16, D), BF16),
            pltpu.VMEM((2, 8, 128), F32),
            pltpu.VMEM((3, 8, 128), F32),
            pltpu.VMEM((3, 8, 128), F32),
            dma((9,)), dma((NS, 9)), dma((NS,)), dma((1,)), dma((NS,)), dma((1,)), dma((NS,)),
            dma((1,)), dma((4, 2)), dma((1,)), dma((4,)), dma((1,)), dma((4,)),
            dma((1,)), dma((4,)), dma((2,)), dma((4, 4)), dma((2,)), dma((2,)), dma((5,)),
        ],
        compiler_params=pltpu.CompilerParams(
            collective_id=0, has_side_effects=True, vmem_limit_bytes=56 << 20
        ),
        cost_estimate=pl.CostEstimate(
            flops=4 * 4096 * 1024 * D, bytes_accessed=4 << 20, transcendentals=4096 * 1024
        ),
    )(points.reshape(2, 128, D), centroids)
    return out.reshape(1024, D), counts.reshape(1024)


def solution(mesh):
    placed = (P(("wide", "narrow"), None), P("narrow", None))
    return jax.shard_map(
        on_device,
        mesh=mesh,
        in_specs=placed,
        out_specs=(P("narrow", None), P("narrow")),
        check_vma=False,
    )
```

time: 101 us -> 97.5 us (0.965); the launches traced: 99.8 us -> 97.3 us
  Pallas kernels: 95.9 us -> 93.4 us
    pallas_call x1, Pallas kernels: 95.9 us -> 93.4 us  [on_device(): pl.pallas_call(kernel, out_shape=(jax.ShapeDtypeStruct((4, 4, 4, 16, D),...]
where the time goes in v2:
time: 97.5 us; the launch traced here: 97.3 us
  Pallas kernels  93.4 us (96%)
  local copies, waits for them, and re-layouts  3.25 us (3%)
    pallas_call x1, Pallas kernels, on_device(): pl.pallas_call(kernel, out_shape=(jax.ShapeDtypeStruct((4, 4, 4, 16, D),...  93.4 us
    unnamed x4, local copies, waits for them, and re-layouts  3.25 us

profile of v2, /device:TPU:8, one launch (start us, length us, event | category | flops | bytes accessed | tf_op | source)
XLA Modules:
  0.0 97.3 jit_solution(10401005950690353504)
XLA Ops:
  0.6 93.4 %shard_map.41 = (bf16[4,4,4,16,768]{4,3,2,1,0:T(8,128)(2,1)}, f32[8,128]{1,0:T(8,128)}) custom-call(bf16[2,128,768]{2,1,0:T(8,128)(2,1)} %bitcast.5, bf16[1024,768]{1,0:T(8,128)(2,1)} %cen_in.1), custom_call_target="tpu_custom_call" | custom-call | flops 12884901888 | bytes 4194304 | tf_op jit(solution)/shard_map/pallas_call | solution.py:419
  94.1 0.0 copy-start
  94.1 2.7 %copy.6 = bf16[1024,768]{1,0:T(8,128)(2,1)} copy(bf16[1024,768]{1,0:T(8,128)(2,1)} %bitcast.3) | data formatting | bytes 3145728
  96.7 0.0 copy-done
  96.7 0.6 copy.7
Async XLA Ops:
  94.1 2.7 %copy-start = (f32[8,128]{1,0:T(8,128)S(1)}, f32[8,128]{1,0:T(8,128)}, u32[]{:S(2)}) copy-start(f32[8,128]{1,0:T(8,128)} %get-tuple-element.5) | copy-start | bytes 12292

commit v3 on v2

v3 whole, which is shorter than its diff:
```python
import functools

import jax
import jax.numpy as jnp
from jax import lax
from jax.experimental import pallas as pl
from jax.experimental.pallas import tpu as pltpu
from jax.sharding import PartitionSpec as P

MESH = pl.DeviceIdType.MESH
F32 = jnp.float32
BF16 = jnp.bfloat16
D = 768
NP = 4
R = 128 // NP
KB = 256
RATE = 60.0 * 1.4426950408889634


def kernel(
    pts_in, cen_in, out_ref, cnt_out,
    pts, cen, e, m_tile, t_tile, s_tile, st_one, st_pair, st_chip, st_up, st_down, st_x, st_z,
    acc, cacc, yb, ry2, rym, zt, zb, rz, outv, cnt, cnt_y, cnt_z,
    x_ss, x_rs, f_ss, f_rs, z_ss, z_rs, s_ss, s_rs, sp_ss, sp_rs, sx_ss, sx_rs, sz_ss, sz_rs, far,
    y2_ss, y2_rs, ym_ss, ym_rs, rz_ss, rz_rs, az_ss, az_rs, ay_ss, ay_rs, c_ss, c_rs, io_sem,
):
    wide, narrow = lax.axis_index("wide"), lax.axis_index("narrow")
    h, y = wide // 4, wide % 4
    zl, x, c = narrow // 8, (narrow // 2) % 4, narrow % 2
    z = 2 * h + zl
    xm, xp, x2 = (x + 3) % 4, (x + 1) % 4, (x + 2) % 4
    ym, yp, y2 = (y + 3) % 4, (y + 1) % 4, (y + 2) % 4

    def at(dx=0, dy=0, dz=0, dc=0):
        zz = (z + dz + 8) % 8
        return (
            (zz // 2) * 4 + (y + dy + 4) % 4,
            (zz % 2) * 8 + ((x + dx + 4) % 4) * 2 + (c + dc) % 2,
        )

    def send(src, dst, ss, rs, device):
        return pltpu.make_async_remote_copy(
            src_ref=src, dst_ref=dst, send_sem=ss, recv_sem=rs, device_id=device, device_id_type=MESH
        )

    def wait(ref, sem):
        send(ref, ref, sem, sem, at(dc=1)).wait_recv()

    cen_copy = pltpu.make_async_copy(cen_in, cen, io_sem.at[0])
    local = pltpu.make_async_copy(pts_in, pts.at[x, pl.ds(0, 2), c], io_sem.at[1])
    cen_copy.start()
    local.start()

    partners = [at(dc=1), at(dx=1), at(dx=-1), at(dy=1), at(dy=-1), at(dz=1), at(dz=-1)]
    barrier = pltpu.get_barrier_semaphore()
    for device in partners:
        pl.semaphore_signal(barrier, inc=1, device_id=device, device_id_type=MESH)
    acc[...] = jnp.zeros_like(acc)
    cacc[...] = jnp.zeros_like(cacc)
    pl.semaphore_wait(barrier, len(partners))

    sources = (x, xm, xp, x2)

    def piece(p):
        return pl.ds(p * R, R)

    def xcopy(p, way):
        return send(
            pts_in.at[:, piece(p)], pts.at[x, pl.ds(0, 2), c, piece(p)],
            x_ss.at[0], x_rs.at[p, way], at(dx=1 - 2 * way),
        )

    def fcopy(p, way):
        block = pts.at[(xm, xp)[way], way, c, piece(p)]
        return send(block, block, f_ss.at[0], f_rs.at[p, way], at(dx=1 - 2 * way))

    def zpoints(p, way, k):
        o = sources[k]
        src = pts_in.at[way, piece(p)] if k == 0 else pts.at[o, way, c, piece(p)]
        return send(src, pts.at[o, 2 + way, c, piece(p)], z_ss.at[0], z_rs.at[k], at(dz=1 - 2 * way))

    def sib(k, p=None):
        o, g = sources[k % 4], 2 * (k // 4)
        rows = pl.ds(0, 128) if p is None else piece(p)
        dst = pts.at[o, pl.ds(g, 2), c, rows]
        return send(pts_in if k == 0 else dst, dst, s_ss.at[0], s_rs.at[k], at(dc=1))

    def sib_arrived(k):
        wait(pts.at[0, pl.ds(0, 2), 0], s_rs.at[k])

    def ev0():
        for p in range(NP):
            for way in range(2):
                xcopy(p, way).start()
                zpoints(p, way, 0).start()
        sib(0).start()

    def ev1(p):
        for way in range(2):
            xcopy(p, way).wait_recv()
        for way in range(2):
            fcopy(p, way).start()
            for k in (1, 2):
                zpoints(p, way, k).start()
        for k in (1, 2):
            sib(k, p).start()

    def ev2(p):
        for way in range(2):
            fcopy(p, way).wait_recv()
            zpoints(p, way, 3).start()
        sib(3, p).start()

    def ev3(k):
        wait(pts.at[0, pl.ds(2, 2), c], z_rs.at[k])
        sib(4 + k).start()

    def mm1(i, g):
        p = pts[i, g].reshape(2 * 128, D)
        for k in range(4):
            l = lax.dot_general(
                cen[k * KB : (k + 1) * KB, :], p, (((1,), (1,)), ((), ())), preferred_element_type=F32
            )
            m = jnp.max(l, axis=0, keepdims=True)
            v = jnp.exp2((l - m) * RATE)
            e[i, g, k * KB : (k + 1) * KB, :] = v
            t = jnp.sum(v, axis=0, keepdims=True)
            for j in range(2):
                m_tile[i, k, pl.ds(2 * ((g + (g + 1) // 2) % 4) + j, 1), :] = m[:, j * 128 : (j + 1) * 128]
                t_tile[i, k, pl.ds(2 * ((g + (g + 1) // 2) % 4) + j, 1), :] = t[:, j * 128 : (j + 1) * 128]

    def merge(parts):
        m = functools.reduce(jnp.maximum, [a for a, _ in parts])
        return m, sum(t * jnp.exp2((a - m) * RATE) for a, t in parts)

    def pair_copy(i):
        return send(st_one.at[i], st_pair.at[i], sp_ss.at[0], sp_rs.at[i], at(dc=1))

    def st_a(i):
        m, t = merge([(m_tile[i, k], t_tile[i, k]) for k in range(4)])
        st_one[i, 0] = m
        st_one[i, 1] = t
        pair_copy(i).start()

    def st_b(i):
        pair_copy(i).wait_recv()
        m, t = merge([(st_one[i, 0], st_one[i, 1]), (st_pair[i, 0], st_pair[i, 1])])
        st_chip[i, 0] = m
        st_chip[i, 1] = t
        st_up[i] = jnp.concatenate([m[2:4], m[0:2], t[2:4], t[0:2]], axis=0)
        st_down[i] = jnp.concatenate([m[6:8], m[4:6], t[6:8], t[4:6]], axis=0)
        for d in (2, 1, 3):
            send(st_chip.at[i], st_x.at[i, d - 1], sx_ss.at[0], sx_rs.at[i], at(dx=d)).start()

    def st_c(i):
        for d in (2, 1, 3, 0):
            send(st_up.at[i], st_z.at[i, 0, d], sz_ss.at[0], sz_rs.at[i], at(dx=d, dz=1)).start()
            send(st_down.at[i], st_z.at[i, 1, d], sz_ss.at[0], sz_rs.at[i], at(dx=d, dz=-1)).start()

    def st_d(i, carry):
        wait(st_x.at[i], sx_rs.at[i])
        wait(st_z.at[i], sz_rs.at[i])
        mine = merge([(st_chip[i, 0], st_chip[i, 1])] + [(st_x[i, d, 0], st_x[i, d, 1]) for d in range(3)])
        far_z = [[(st_z[i, w, d][:4], st_z[i, w, d][4:]) for d in range(4)] for w in (1, 0)]
        above, below = merge(far_z[0]), merge(far_z[1])
        other = [jnp.concatenate([a, b], axis=0) for a, b in zip(above, below)]
        m, t = merge([mine, tuple(other)])
        inv = 1.0 / t
        for k in range(4):
            s_tile[i, k] = jnp.exp2((m_tile[i, k] - m) * RATE) * inv
        return carry

    ev0()
    cen_copy.wait()
    local.wait()

    def step(t, carry):
        def before(n, *acts):
            @pl.when(t == n)
            def _():
                for act in acts:
                    act()

        def do(f, *a):
            return functools.partial(f, *a)

        before(0, do(sib_arrived, 0))
        before(1, do(ev1, 0))
        before(2, do(ev1, 1), do(ev3, 0), do(ev1, 2), do(sib_arrived, 4))
        before(4, do(st_a, x), do(ev1, 3), do(ev2, 0), do(sib_arrived, 1))
        before(5, do(ev2, 1), do(st_b, x))
        before(6, do(ev2, 2), do(sib_arrived, 2))
        before(7, do(ev2, 3), do(ev3, 1))
        before(8, do(sib_arrived, 5))
        before(9, do(ev3, 2))
        before(10, do(st_a, xm), do(sib_arrived, 6))
        before(12, do(st_a, xp), do(st_b, xm), do(sib_arrived, 3))
        before(13, do(st_b, xp))
        before(14, do(ev3, 3), do(st_c, x), do(st_c, xm), do(st_c, xp), do(sib_arrived, 7))
        j = t // 4
        mid = (j % 3 + 1) // 2
        off = mid * (3 - 2 * ((t % 4) // 2)) + (1 - mid) * (2 * (j // 3))
        g = mid * ((j - 1) * 2 + t % 2) + (1 - mid) * (t % 4)
        mm1((x + off) % 4, g)
        return carry

    lax.fori_loop(0, 16, step, 0)
    st_a(x2)
    st_b(x2)
    st_c(x2)
    lax.fori_loop(0, 4, st_d, 0)
    for d in (2, -2):
        pl.semaphore_signal(far, inc=1, device_id=at(dz=d), device_id_type=MESH)

    def mm2(n, lo, hi):
        def part(i, carry):
            cs = jnp.zeros((KB, 128), F32)
            resp = []
            for g in range(4):
                for j in range(2):
                    v = e[i, g, n * KB : (n + 1) * KB, j * 128 : (j + 1) * 128]
                    v = v * s_tile[i, n, pl.ds(2 * ((g + (g + 1) // 2) % 4) + j, 1), :]
                    cs = cs + v
                    resp.append(v.astype(BF16))
            cacc[n * KB : (n + 1) * KB, :] += cs
            acc[n] += jnp.dot(
                jnp.concatenate(resp, axis=1), pts[i].reshape(1024, D), preferred_element_type=F32
            ).reshape(4, 64, D)
            return carry

        lax.fori_loop(lo, hi, part, 0)

    def cols(side):
        return pl.ds(side * (D // 2), D // 2)

    def ycopy(n, kind, side):
        to, near = at(dy=1 - 2 * side), (yp, ym)[side]
        if kind == 0:
            return send(yb.at[n, y2, :, cols(side)], ry2.at[n, side], y2_ss.at[0], y2_rs.at[n, side], to)
        part = cols(1 - side if kind == 1 else side)
        return send(yb.at[n, near, :, part], rym.at[n, side, :, part], ym_ss.at[0], ym_rs.at[n], to)

    def rs_a(n):
        yb[n] = acc[n].astype(BF16)
        for kind in range(2):
            for side in range(2):
                ycopy(n, kind, side).start()

    def rs_b(n):
        for side, near in ((0, yp), (1, ym)):
            ycopy(n, 0, side).wait_recv()
            part = cols(side)
            yb[n, near, :, part] = (acc[n, near, :, part] + ry2[n, side].astype(F32)).astype(BF16)
            ycopy(n, 2, side).start()

    def zcopy(n, d):
        return send(zb.at[n, (h + d) % 4], rz.at[n, d - 1], rz_ss.at[0], rz_rs.at[n], at(dz=2 * d))

    def rs_c(n):
        wait(rym.at[n], ym_rs.at[n])
        total = acc[n, y] + rym[n, 0].astype(F32) + rym[n, 1].astype(F32)
        zt[n] = total.reshape(4, 16, D)
        zb[n] = total.astype(BF16).reshape(4, 16, D)
        if n == 0:
            pl.semaphore_wait(far, 2)
        for d in (2, 1, 3):
            zcopy(n, d).start()

    def azcopy(n, d):
        return send(outv.at[n, y, h], outv.at[n, y, h], az_ss.at[0], az_rs.at[n], at(dz=2 * d))

    def aycopy(n, q):
        side = q % 2
        to, ss, rs = at(dy=1 - 2 * side), ay_ss.at[q // 2], ay_rs.at[n, q]
        block = outv.at[n, y] if q < 2 else outv.at[n, (ym, yp)[side], :, :, cols(side)]
        return send(block, block, ss, rs, to)

    def writeback(n):
        return pltpu.make_async_copy(outv.at[n], out_ref.at[n], io_sem.at[2 + n])

    def ag_f(n):
        wait(rz.at[n], rz_rs.at[n])
        total = zt[n, h]
        for d in range(3):
            total = total + rz[n, d].astype(F32)
        scale = lax.rsqrt(jnp.sum(total * total, axis=1, keepdims=True) + 1e-06)
        outv[n, y, h] = (total * scale).astype(BF16)
        for d in (2, 1, 3):
            azcopy(n, d).start()

    def ag_g(n):
        wait(rz.at[n], az_rs.at[n])
        for q in range(2):
            aycopy(n, q).start()

    def ag_h(n):
        for q in range(2):
            aycopy(n, q).wait_recv()
            aycopy(n, 2 + q).start()

    def ag_i(n):
        for q in range(2, 4):
            aycopy(n, q).wait_recv()
        writeback(n).start()

    def ccopy(n):
        d = n % 3 + 1
        if n < 3:
            return send(cnt.at[0], cnt_y.at[d - 1], c_ss.at[0], c_rs.at[0], at(dy=d))
        return send(cnt.at[1], cnt_z.at[d - 1], c_ss.at[1], c_rs.at[1], at(dz=2 * d))

    def cnt_a():
        rest, lanes = cacc[...], jnp.zeros((8, 1024), F32)
        ones = jnp.ones((8, 128), BF16)
        for _ in range(3):
            term = rest.astype(BF16)
            lanes += lax.dot_general(ones, term, (((1,), (1,)), ((), ())), preferred_element_type=F32)
            rest = rest - term.astype(F32)
        row = lax.broadcasted_iota(jnp.int32, (8, 128), 0)
        dense = jnp.zeros((8, 128), F32)
        for r in range(8):
            dense = jnp.where(row == r, lanes[:, r * 128 : (r + 1) * 128], dense)
        cnt[0] = dense
        for n in range(3):
            ccopy(n).start()

    def cnt_b():
        wait(cnt_y, c_rs.at[0])
        cnt[1] = cnt[0] + cnt_y[0] + cnt_y[1] + cnt_y[2]
        for n in range(3, 6):
            ccopy(n).start()

    def cnt_c():
        wait(cnt_z, c_rs.at[1])
        cnt_out[...] = cnt[1] + cnt_z[0] + cnt_z[1] + cnt_z[2]

    mm2(0, 0, 4)
    rs_a(0)
    mm2(1, 0, 4)
    rs_a(1)
    rs_b(0)
    mm2(2, 0, 4)
    rs_a(2)
    rs_b(1)
    rs_c(0)
    mm2(3, 0, 4)
    rs_a(3)
    rs_b(2)
    rs_c(1)
    ag_f(0)
    rs_b(3)
    rs_c(2)
    ag_f(1)
    ag_g(0)
    rs_c(3)
    cnt_a()
    ag_f(2)
    ag_g(1)
    ag_h(0)
    ag_f(3)
    ag_g(2)
    cnt_b()
    ag_i(0)
    ag_h(1)
    ag_g(3)
    ag_i(1)
    ag_h(2)
    cnt_c()
    ag_i(2)
    ag_h(3)
    ag_i(3)

    wait(pts.at[0, pl.ds(0, 2)], x_ss.at[0])
    wait(pts.at[0, 0], f_ss.at[0])
    wait(pts.at[0], z_ss.at[0])
    wait(pts.at[pl.ds(0, 2)], s_ss.at[0])
    wait(st_pair, sp_ss.at[0])
    wait(st_x, sx_ss.at[0])
    wait(st_z, sz_ss.at[0])
    wait(ry2, y2_ss.at[0])
    wait(rym, ym_ss.at[0])
    wait(rz, rz_ss.at[0])
    wait(rz, az_ss.at[0])
    wait(outv.at[pl.ds(0, 2)], ay_ss.at[0])
    wait(outv.at[0], ay_ss.at[1])
    wait(cnt_y, c_ss.at[0])
    wait(cnt_z, c_ss.at[1])
    for n in range(4):
        writeback(n).wait()


def on_device(points, centroids):
    dma = pltpu.SemaphoreType.DMA
    out, counts = pl.pallas_call(
        kernel,
        out_shape=(
            jax.ShapeDtypeStruct((4, 4, 4, 16, D), BF16),
            jax.ShapeDtypeStruct((8, 128), F32),
        ),
        in_specs=[pl.BlockSpec(memory_space=pl.ANY)] * 2,
        out_specs=(
            pl.BlockSpec(memory_space=pl.ANY),
            pl.BlockSpec(memory_space=pltpu.VMEM),
        ),
        scratch_shapes=[
            pltpu.VMEM((4, 4, 2, 128, D), BF16),
            pltpu.VMEM((1024, D), BF16),
            pltpu.VMEM((4, 4, 1024, 256), F32),
            pltpu.VMEM((4, 4, 8, 128), F32),
            pltpu.VMEM((4, 4, 8, 128), F32),
            pltpu.VMEM((4, 4, 8, 128), F32),
            pltpu.VMEM((4, 2, 8, 128), F32),
            pltpu.VMEM((4, 2, 8, 128), F32),
            pltpu.VMEM((4, 2, 8, 128), F32),
            pltpu.VMEM((4, 8, 128), F32),
            pltpu.VMEM((4, 8, 128), F32),
            pltpu.VMEM((4, 3, 2, 8, 128), F32),
            pltpu.VMEM((4, 2, 4, 8, 128), F32),
            pltpu.VMEM((4, 4, 64, D), F32),
            pltpu.VMEM((1024, 128), F32),
            pltpu.VMEM((4, 4, 64, D), BF16),
            pltpu.VMEM((4, 2, 64, D // 2), BF16),
            pltpu.VMEM((4, 2, 64, D), BF16),
            pltpu.VMEM((4, 4, 16, D), F32),
            pltpu.VMEM((4, 4, 16, D), BF16),
            pltpu.VMEM((4, 3, 16, D), BF16),
            pltpu.VMEM((4, 4, 4, 16, D), BF16),
            pltpu.VMEM((2, 8, 128), F32),
            pltpu.VMEM((3, 8, 128), F32),
            pltpu.VMEM((3, 8, 128), F32),
            dma((1,)), dma((NP, 2)), dma((1,)), dma((NP, 2)), dma((1,)), dma((4,)), dma((1,)), dma((8,)),
            dma((1,)), dma((4,)), dma((1,)), dma((4,)), dma((1,)), dma((4,)), pltpu.SemaphoreType.REGULAR,
            dma((1,)), dma((4, 2)), dma((1,)), dma((4,)), dma((1,)), dma((4,)),
            dma((1,)), dma((4,)), dma((2,)), dma((4, 4)), dma((2,)), dma((2,)), dma((6,)),
        ],
        compiler_params=pltpu.CompilerParams(
            collective_id=0, has_side_effects=True, vmem_limit_bytes=56 << 20
        ),
        cost_estimate=pl.CostEstimate(
            flops=4 * 4096 * 1024 * D, bytes_accessed=4 << 20, transcendentals=4096 * 1024
        ),
    )(points.reshape(2, 128, D), centroids)
    return out.reshape(1024, D), counts.reshape(1024)


def solution(mesh):
    placed = (P(("wide", "narrow"), None), P("narrow", None))
    return jax.shard_map(
        on_device,
        mesh=mesh,
        in_specs=placed,
        out_specs=(P("narrow", None), P("narrow")),
        check_vma=False,
    )
```

time: 97.5 us -> 89.5 us (0.918)
  Pallas kernels: 93.4 us -> 85 us
    pallas_call x1, Pallas kernels: 93.4 us -> 85 us  [on_device(): pl.pallas_call(kernel, out_shape=(jax.ShapeDtypeStruct((4, 4, 4, 16, D),...]
where the time goes in v3:
time: 89.5 us; the launch traced here: 88.9 us
  Pallas kernels  85 us (95%)
  local copies, waits for them, and re-layouts  3.25 us (4%)
    pallas_call x1, Pallas kernels, on_device(): pl.pallas_call(kernel, out_shape=(jax.ShapeDtypeStruct((4, 4, 4, 16, D),...  85 us
    unnamed x4, local copies, waits for them, and re-layouts  3.25 us

profile of v3, /device:TPU:8, one launch (start us, length us, event | category | flops | bytes accessed | tf_op | source)
XLA Modules:
  0.0 88.9 jit_solution(16136101937540148205)
XLA Ops:
  0.6 85.0 %shard_map.41 = (bf16[4,4,4,16,768]{4,3,2,1,0:T(8,128)(2,1)}, f32[8,128]{1,0:T(8,128)}) custom-call(bf16[2,128,768]{2,1,0:T(8,128)(2,1)} %bitcast.5, bf16[1024,768]{1,0:T(8,128)(2,1)} %cen_in.1), custom_call_target="tpu_custom_call" | custom-call | flops 12884901888 | bytes 4194304 | tf_op jit(solution)/shard_map/pallas_call | solution.py:394
  85.7 0.0 copy-start
  85.7 2.7 %copy.6 = bf16[1024,768]{1,0:T(8,128)(2,1)} copy(bf16[1024,768]{1,0:T(8,128)(2,1)} %bitcast.3) | data formatting | bytes 3145728
  88.3 0.0 copy-done
  88.3 0.6 copy.7
Async XLA Ops:
  85.7 2.7 %copy-start = (f32[8,128]{1,0:T(8,128)S(1)}, f32[8,128]{1,0:T(8,128)}, u32[]{:S(2)}) copy-start(f32[8,128]{1,0:T(8,128)} %get-tuple-element.5) | copy-start | bytes 12292

commit v4 on v3

--- a/solution.py
+++ b/solution.py
@@ -115,19 +115,23 @@
         wait(pts.at[0, pl.ds(2, 2), c], z_rs.at[k])
         sib(4 + k).start()
 
-    def mm1(i, g):
-        p = pts[i, g].reshape(2 * 128, D)
+    def mm1(i, w):
+        p = pts[i, pl.ds(2 * w, 2)].reshape(512, D)
         for k in range(4):
             l = lax.dot_general(
                 cen[k * KB : (k + 1) * KB, :], p, (((1,), (1,)), ((), ())), preferred_element_type=F32
             )
             m = jnp.max(l, axis=0, keepdims=True)
             v = jnp.exp2((l - m) * RATE)
-            e[i, g, k * KB : (k + 1) * KB, :] = v
             t = jnp.sum(v, axis=0, keepdims=True)
-            for j in range(2):
-                m_tile[i, k, pl.ds(2 * ((g + (g + 1) // 2) % 4) + j, 1), :] = m[:, j * 128 : (j + 1) * 128]
-                t_tile[i, k, pl.ds(2 * ((g + (g + 1) // 2) % 4) + j, 1), :] = t[:, j * 128 : (j + 1) * 128]
+            for q in range(2):
+                g = 2 * w + q
+                e[i, g, k * KB : (k + 1) * KB, :] = v[:, q * 256 : (q + 1) * 256]
+                for j in range(2):
+                    row = pl.ds(2 * ((g + (g + 1) // 2) % 4) + j, 1)
+                    lanes = slice(q * 256 + j * 128, q * 256 + (j + 1) * 128)
+                    m_tile[i, k, row, :] = m[:, lanes]
+                    t_tile[i, k, row, :] = t[:, lanes]
 
     def merge(parts):
         m = functools.reduce(jnp.maximum, [a for a, _ in parts])
@@ -185,26 +189,20 @@
             return functools.partial(f, *a)
 
         before(0, do(sib_arrived, 0))
-        before(1, do(ev1, 0))
-        before(2, do(ev1, 1), do(ev3, 0), do(ev1, 2), do(sib_arrived, 4))
-        before(4, do(st_a, x), do(ev1, 3), do(ev2, 0), do(sib_arrived, 1))
-        before(5, do(ev2, 1), do(st_b, x))
-        before(6, do(ev2, 2), do(sib_arrived, 2))
-        before(7, do(ev2, 3), do(ev3, 1))
-        before(8, do(sib_arrived, 5))
-        before(9, do(ev3, 2))
-        before(10, do(st_a, xm), do(sib_arrived, 6))
-        before(12, do(st_a, xp), do(st_b, xm), do(sib_arrived, 3))
-        before(13, do(st_b, xp))
-        before(14, do(ev3, 3), do(st_c, x), do(st_c, xm), do(st_c, xp), do(sib_arrived, 7))
-        j = t // 4
+        before(1, do(ev1, 0), do(ev1, 1), do(ev3, 0), do(ev1, 2), do(sib_arrived, 4))
+        before(2, do(st_a, x), do(ev1, 3), do(ev2, 0), do(sib_arrived, 1))
+        before(3, do(ev2, 1), do(sib_arrived, 2), do(st_b, x))
+        before(4, do(ev2, 2), do(ev2, 3), do(ev3, 1), do(ev3, 2), do(sib_arrived, 5))
+        before(5, do(st_a, xm), do(sib_arrived, 6))
+        before(6, do(st_a, xp), do(st_b, xm), do(ev3, 3), do(sib_arrived, 3))
+        before(7, do(st_b, xp), do(st_c, x), do(st_c, xm), do(st_c, xp), do(sib_arrived, 7))
+        j = t // 2
         mid = (j % 3 + 1) // 2
-        off = mid * (3 - 2 * ((t % 4) // 2)) + (1 - mid) * (2 * (j // 3))
-        g = mid * ((j - 1) * 2 + t % 2) + (1 - mid) * (t % 4)
-        mm1((x + off) % 4, g)
+        off = mid * (3 - 2 * (t % 2)) + (1 - mid) * (2 * (j // 3))
+        mm1((x + off) % 4, mid * (j - 1) + (1 - mid) * (t % 2))
         return carry
 
-    lax.fori_loop(0, 16, step, 0)
+    lax.fori_loop(0, 8, step, 0)
     st_a(x2)
     st_b(x2)
     st_c(x2)
@@ -351,23 +349,23 @@
     rs_b(3)
     rs_c(2)
     ag_f(1)
+    rs_c(3)
     ag_g(0)
-    rs_c(3)
+    ag_f(2)
     cnt_a()
-    ag_f(2)
     ag_g(1)
     ag_h(0)
     ag_f(3)
     ag_g(2)
+    ag_h(1)
     cnt_b()
+    ag_g(3)
+    ag_h(2)
+    ag_h(3)
+    cnt_c()
     ag_i(0)
-    ag_h(1)
-    ag_g(3)
     ag_i(1)
-    ag_h(2)
-    cnt_c()
     ag_i(2)
-    ag_h(3)
     ag_i(3)
 
     wait(pts.at[0, pl.ds(0, 2)], x_ss.at[0])

time: 89.5 us -> 81.7 us (0.913)
  Pallas kernels: 85 us -> 77.7 us
    pallas_call x1, Pallas kernels: 85 us -> 77.7 us  [on_device(): pl.pallas_call(kernel, out_shape=(jax.ShapeDtypeStruct((4, 4, 4, 16, D),...]
where the time goes in v4:
time: 81.7 us; the launch traced here: 81.6 us
  Pallas kernels  77.7 us (95%)
  local copies, waits for them, and re-layouts  3.25 us (4%)
    pallas_call x1, Pallas kernels, on_device(): pl.pallas_call(kernel, out_shape=(jax.ShapeDtypeStruct((4, 4, 4, 16, D),...  77.7 us
    unnamed x4, local copies, waits for them, and re-layouts  3.25 us

profile of v4, /device:TPU:8, one launch (start us, length us, event | category | flops | bytes accessed | tf_op | source)
XLA Modules:
  0.0 81.6 jit_solution(4648525010590756052)
XLA Ops:
  0.6 77.7 %shard_map.41 = (bf16[4,4,4,16,768]{4,3,2,1,0:T(8,128)(2,1)}, f32[8,128]{1,0:T(8,128)}) custom-call(bf16[2,128,768]{2,1,0:T(8,128)(2,1)} %bitcast.5, bf16[1024,768]{1,0:T(8,128)(2,1)} %cen_in.1), custom_call_target="tpu_custom_call" | custom-call | flops 12884901888 | bytes 4194304 | tf_op jit(solution)/shard_map/pallas_call | solution.py:392
  78.3 0.0 copy-start
  78.3 2.7 %copy.6 = bf16[1024,768]{1,0:T(8,128)(2,1)} copy(bf16[1024,768]{1,0:T(8,128)(2,1)} %bitcast.3) | data formatting | bytes 3145728
  81.0 0.0 copy-done
  81.0 0.6 copy.7
Async XLA Ops:
  78.3 2.7 %copy-start = (f32[8,128]{1,0:T(8,128)S(1)}, f32[8,128]{1,0:T(8,128)}, u32[]{:S(2)}) copy-start(f32[8,128]{1,0:T(8,128)} %get-tuple-element.5) | copy-start | bytes 12292

commit v5 on v4

--- a/solution.py
+++ b/solution.py
@@ -18,9 +18,9 @@
 
 
 def kernel(
-    pts_in, cen_in, out_ref, cnt_out,
+    pts_in, cen_in, outv, cnt_out,
     pts, cen, e, m_tile, t_tile, s_tile, st_one, st_pair, st_chip, st_up, st_down, st_x, st_z,
-    acc, cacc, yb, ry2, rym, zt, zb, rz, outv, cnt, cnt_y, cnt_z,
+    acc, cacc, yb, ry2, rym, zt, zb, rz, cnt, cnt_y, cnt_z,
     x_ss, x_rs, f_ss, f_rs, z_ss, z_rs, s_ss, s_rs, sp_ss, sp_rs, sx_ss, sx_rs, sz_ss, sz_rs, far,
     y2_ss, y2_rs, ym_ss, ym_rs, rz_ss, rz_rs, az_ss, az_rs, ay_ss, ay_rs, c_ss, c_rs, io_sem,
 ):
@@ -273,9 +273,6 @@
         block = outv.at[n, y] if q < 2 else outv.at[n, (ym, yp)[side], :, :, cols(side)]
         return send(block, block, ss, rs, to)
 
-    def writeback(n):
-        return pltpu.make_async_copy(outv.at[n], out_ref.at[n], io_sem.at[2 + n])
-
     def ag_f(n):
         wait(rz.at[n], rz_rs.at[n])
         total = zt[n, h]
@@ -299,7 +296,6 @@
     def ag_i(n):
         for q in range(2, 4):
             aycopy(n, q).wait_recv()
-        writeback(n).start()
 
     def ccopy(n):
         d = n % 3 + 1
@@ -383,8 +379,6 @@
     wait(outv.at[0], ay_ss.at[1])
     wait(cnt_y, c_ss.at[0])
     wait(cnt_z, c_ss.at[1])
-    for n in range(4):
-        writeback(n).wait()
 
 
 def on_device(points, centroids):
@@ -396,10 +390,7 @@
             jax.ShapeDtypeStruct((8, 128), F32),
         ),
         in_specs=[pl.BlockSpec(memory_space=pl.ANY)] * 2,
-        out_specs=(
-            pl.BlockSpec(memory_space=pl.ANY),
-            pl.BlockSpec(memory_space=pltpu.VMEM),
-        ),
+        out_specs=[pl.BlockSpec(memory_space=pltpu.VMEM)] * 2,
         scratch_shapes=[
             pltpu.VMEM((4, 4, 2, 128, D), BF16),
             pltpu.VMEM((1024, D), BF16),
@@ -422,17 +413,16 @@
             pltpu.VMEM((4, 4, 16, D), F32),
             pltpu.VMEM((4, 4, 16, D), BF16),
             pltpu.VMEM((4, 3, 16, D), BF16),
-            pltpu.VMEM((4, 4, 4, 16, D), BF16),
             pltpu.VMEM((2, 8, 128), F32),
             pltpu.VMEM((3, 8, 128), F32),
             pltpu.VMEM((3, 8, 128), F32),
             dma((1,)), dma((NP, 2)), dma((1,)), dma((NP, 2)), dma((1,)), dma((4,)), dma((1,)), dma((8,)),
             dma((1,)), dma((4,)), dma((1,)), dma((4,)), dma((1,)), dma((4,)), pltpu.SemaphoreType.REGULAR,
             dma((1,)), dma((4, 2)), dma((1,)), dma((4,)), dma((1,)), dma((4,)),
-            dma((1,)), dma((4,)), dma((2,)), dma((4, 4)), dma((2,)), dma((2,)), dma((6,)),
+            dma((1,)), dma((4,)), dma((2,)), dma((4, 4)), dma((2,)), dma((2,)), dma((2,)),
         ],
         compiler_params=pltpu.CompilerParams(
-            collective_id=0, has_side_effects=True, vmem_limit_bytes=56 << 20
+            collective_id=0, has_side_effects=True, vmem_limit_bytes=51 << 20
         ),
         cost_estimate=pl.CostEstimate(
             flops=4 * 4096 * 1024 * D, bytes_accessed=4 << 20, transcendentals=4096 * 1024

time: 81.7 us -> 79.9 us (0.978)
  Pallas kernels: 77.7 us -> 76.4 us
    pallas_call x1, Pallas kernels: 77.7 us -> 76.4 us  [on_device(): pl.pallas_call(kernel, out_shape=(jax.ShapeDtypeStruct((4, 4, 4, 16, D),...]
where the time goes in v5:
time: 79.9 us; the launch traced here: 79.8 us
  Pallas kernels  76.4 us (96%)
  local copies, waits for them, and re-layouts  2.73 us (3%)
    pallas_call x1, Pallas kernels, on_device(): pl.pallas_call(kernel, out_shape=(jax.ShapeDtypeStruct((4, 4, 4, 16, D),...  76.4 us
    unnamed x4, local copies, waits for them, and re-layouts  2.73 us

profile of v5, /device:TPU:8, one launch (start us, length us, event | category | flops | bytes accessed | tf_op | source)
XLA Modules:
  0.0 79.8 jit_solution(5862444900187983718)
XLA Ops:
  0.6 0.0 copy-start
  0.6 1.0 %copy-done = bf16[256,768]{1,0:T(8,128)(2,1)S(1)} copy-done((bf16[256,768]{1,0:T(8,128)(2,1)S(1)}, bf16[256,768]{1,0:T(8,128)(2,1)}, u32[]{:S(2)}) %copy-start) | copy-done | bytes 393240
  1.6 76.4 %shard_map.41 = (bf16[4,4,4,16,768]{4,3,2,1,0:T(8,128)(2,1)S(1)}, f32[8,128]{1,0:T(8,128)S(1)}) custom-call(bf16[2,128,768]{2,1,0:T(8,128)(2,1)S(1)} %bitcast.5, bf16[1024,768]{1,0:T(8,128)(2,1)} %cen_in.1), custom_call_target="tpu_custom_call" | custom-call | flops 12884901888 | bytes 4194304 | tf_op jit(solution)/shard_map/pallas_call | solution.py:386
  78.0 1.1 %copy.6 = bf16[1024,768]{1,0:T(8,128)(2,1)} copy(bf16[1024,768]{1,0:T(8,128)(2,1)S(1)} %bitcast.3) | data formatting | bytes 3145728
  79.2 0.6 copy.7
Async XLA Ops:
  0.6 1.0 %copy-start = (bf16[256,768]{1,0:T(8,128)(2,1)S(1)}, bf16[256,768]{1,0:T(8,128)(2,1)}, u32[]{:S(2)}) copy-start(bf16[256,768]{1,0:T(8,128)(2,1)} %param.2) | copy-start | bytes 1179652

commit v6 on v5

--- a/solution.py
+++ b/solution.py
@@ -55,8 +55,6 @@
     barrier = pltpu.get_barrier_semaphore()
     for device in partners:
         pl.semaphore_signal(barrier, inc=1, device_id=device, device_id_type=MESH)
-    acc[...] = jnp.zeros_like(acc)
-    cacc[...] = jnp.zeros_like(cacc)
     pl.semaphore_wait(barrier, len(partners))
 
     sources = (x, xm, xp, x2)
@@ -153,6 +151,8 @@
         st_chip[i, 1] = t
         st_up[i] = jnp.concatenate([m[2:4], m[0:2], t[2:4], t[0:2]], axis=0)
         st_down[i] = jnp.concatenate([m[6:8], m[4:6], t[6:8], t[4:6]], axis=0)
+
+    def st_x_send(i):
         for d in (2, 1, 3):
             send(st_chip.at[i], st_x.at[i, d - 1], sx_ss.at[0], sx_rs.at[i], at(dx=d)).start()
 
@@ -191,11 +191,11 @@
         before(0, do(sib_arrived, 0))
         before(1, do(ev1, 0), do(ev1, 1), do(ev3, 0), do(ev1, 2), do(sib_arrived, 4))
         before(2, do(st_a, x), do(ev1, 3), do(ev2, 0), do(sib_arrived, 1))
-        before(3, do(ev2, 1), do(sib_arrived, 2), do(st_b, x))
+        before(3, do(ev2, 1), do(sib_arrived, 2), do(st_b, x), do(st_x_send, x))
         before(4, do(ev2, 2), do(ev2, 3), do(ev3, 1), do(ev3, 2), do(sib_arrived, 5))
         before(5, do(st_a, xm), do(sib_arrived, 6))
-        before(6, do(st_a, xp), do(st_b, xm), do(ev3, 3), do(sib_arrived, 3))
-        before(7, do(st_b, xp), do(st_c, x), do(st_c, xm), do(st_c, xp), do(sib_arrived, 7))
+        before(6, do(st_a, xp), do(st_b, xm), do(st_x_send, xm), do(ev3, 3), do(sib_arrived, 3))
+        before(7, do(st_b, xp), do(st_x_send, xp), do(st_c, x), do(st_c, xm), do(st_c, xp), do(sib_arrived, 7))
         j = t // 2
         mid = (j % 3 + 1) // 2
         off = mid * (3 - 2 * (t % 2)) + (1 - mid) * (2 * (j // 3))
@@ -206,27 +206,27 @@
     st_a(x2)
     st_b(x2)
     st_c(x2)
+    st_x_send(x2)
     lax.fori_loop(0, 4, st_d, 0)
     for d in (2, -2):
         pl.semaphore_signal(far, inc=1, device_id=at(dz=d), device_id_type=MESH)
 
-    def mm2(n, lo, hi):
-        def part(i, carry):
-            cs = jnp.zeros((KB, 128), F32)
-            resp = []
+    def mm2(n):
+        rows = pl.ds(pl.multiple_of(n * KB, KB), KB)
+
+        cs = jnp.zeros((KB, 128), F32)
+        resp = []
+        for i in range(4):
             for g in range(4):
                 for j in range(2):
-                    v = e[i, g, n * KB : (n + 1) * KB, j * 128 : (j + 1) * 128]
-                    v = v * s_tile[i, n, pl.ds(2 * ((g + (g + 1) // 2) % 4) + j, 1), :]
+                    row = 2 * ((g + (g + 1) // 2) % 4) + j
+                    v = e[i, g, rows, j * 128 : (j + 1) * 128] * s_tile[i, n, row : row + 1, :]
                     cs = cs + v
                     resp.append(v.astype(BF16))
-            cacc[n * KB : (n + 1) * KB, :] += cs
-            acc[n] += jnp.dot(
-                jnp.concatenate(resp, axis=1), pts[i].reshape(1024, D), preferred_element_type=F32
-            ).reshape(4, 64, D)
-            return carry
-
-        lax.fori_loop(lo, hi, part, 0)
+        cacc[rows, :] = cs
+        acc[n] = jnp.dot(
+            jnp.concatenate(resp, axis=1), pts[...].reshape(4096, D), preferred_element_type=F32
+        ).reshape(4, 64, D)
 
     def cols(side):
         return pl.ds(side * (D // 2), D // 2)
@@ -259,8 +259,11 @@
         total = acc[n, y] + rym[n, 0].astype(F32) + rym[n, 1].astype(F32)
         zt[n] = total.reshape(4, 16, D)
         zb[n] = total.astype(BF16).reshape(4, 16, D)
-        if n == 0:
+
+        @pl.when(n == 0)
+        def _():
             pl.semaphore_wait(far, 2)
+
         for d in (2, 1, 3):
             zcopy(n, d).start()
 
@@ -328,41 +331,27 @@
         wait(cnt_z, c_rs.at[1])
         cnt_out[...] = cnt[1] + cnt_z[0] + cnt_z[1] + cnt_z[2]
 
-    mm2(0, 0, 4)
-    rs_a(0)
-    mm2(1, 0, 4)
-    rs_a(1)
-    rs_b(0)
-    mm2(2, 0, 4)
-    rs_a(2)
-    rs_b(1)
-    rs_c(0)
-    mm2(3, 0, 4)
-    rs_a(3)
-    rs_b(2)
-    rs_c(1)
-    ag_f(0)
-    rs_b(3)
-    rs_c(2)
-    ag_f(1)
-    rs_c(3)
-    ag_g(0)
-    ag_f(2)
-    cnt_a()
-    ag_g(1)
-    ag_h(0)
-    ag_f(3)
-    ag_g(2)
-    ag_h(1)
-    cnt_b()
-    ag_g(3)
-    ag_h(2)
-    ag_h(3)
+    def wave(s, carry):
+        def chunk(lag, *acts):
+            @pl.when((s >= lag) & (s < lag + 4))
+            def _():
+                for act in acts:
+                    act(s - lag)
+
+        chunk(0, mm2, rs_a)
+        chunk(4, ag_f)
+        chunk(1, rs_b)
+        chunk(2, rs_c)
+        chunk(5, ag_g)
+        pl.when(s == 6)(cnt_a)
+        chunk(6, ag_h)
+        pl.when(s == 7)(cnt_b)
+        return carry
+
+    lax.fori_loop(0, 10, wave, 0)
     cnt_c()
-    ag_i(0)
-    ag_i(1)
-    ag_i(2)
-    ag_i(3)
+    for n in range(4):
+        ag_i(n)
 
     wait(pts.at[0, pl.ds(0, 2)], x_ss.at[0])
     wait(pts.at[0, 0], f_ss.at[0])

time: 79.9 us -> 79.3 us (level)
  no operation moved by 1% of the time
where the time goes in v6:
time: 79.3 us; the launch traced here: 79.2 us
  Pallas kernels  75.8 us (96%)
  local copies, waits for them, and re-layouts  2.73 us (3%)
    pallas_call x1, Pallas kernels, on_device(): pl.pallas_call(kernel, out_shape=(jax.ShapeDtypeStruct((4, 4, 4, 16, D),...  75.8 us
    unnamed x4, local copies, waits for them, and re-layouts  2.73 us

profile of v6, /device:TPU:8, one launch (start us, length us, event | category | flops | bytes accessed | tf_op | source)
XLA Modules:
  0.0 79.2 jit_solution(5201885215495743095)
XLA Ops:
  0.6 0.0 copy-start
  0.6 1.0 %copy-done = bf16[256,768]{1,0:T(8,128)(2,1)S(1)} copy-done((bf16[256,768]{1,0:T(8,128)(2,1)S(1)}, bf16[256,768]{1,0:T(8,128)(2,1)}, u32[]{:S(2)}) %copy-start) | copy-done | bytes 393240
  1.6 75.8 %shard_map.41 = (bf16[4,4,4,16,768]{4,3,2,1,0:T(8,128)(2,1)S(1)}, f32[8,128]{1,0:T(8,128)S(1)}) custom-call(bf16[2,128,768]{2,1,0:T(8,128)(2,1)S(1)} %bitcast.5, bf16[1024,768]{1,0:T(8,128)(2,1)} %cen_in.1), custom_call_target="tpu_custom_call" | custom-call | flops 12884901888 | bytes 4194304 | tf_op jit(solution)/shard_map/pallas_call | solution.py:375
  77.5 1.1 %copy.6 = bf16[1024,768]{1,0:T(8,128)(2,1)} copy(bf16[1024,768]{1,0:T(8,128)(2,1)S(1)} %bitcast.3) | data formatting | bytes 3145728
  78.6 0.6 copy.7
Async XLA Ops:
  0.6 1.0 %copy-start = (bf16[256,768]{1,0:T(8,128)(2,1)S(1)}, bf16[256,768]{1,0:T(8,128)(2,1)}, u32[]{:S(2)}) copy-start(bf16[256,768]{1,0:T(8,128)(2,1)} %param.2) | copy-start | bytes 1179652

commit v7 on v6

--- a/solution.py
+++ b/solution.py
@@ -25,18 +25,20 @@
     y2_ss, y2_rs, ym_ss, ym_rs, rz_ss, rz_rs, az_ss, az_rs, ay_ss, ay_rs, c_ss, c_rs, io_sem,
 ):
     wide, narrow = lax.axis_index("wide"), lax.axis_index("narrow")
-    h, y = wide // 4, wide % 4
-    zl, x, c = narrow // 8, (narrow // 2) % 4, narrow % 2
+    h, y = lax.div(wide, 4), lax.rem(wide, 4)
+    zl, x, c = lax.div(narrow, 8), lax.rem(lax.div(narrow, 2), 4), lax.rem(narrow, 2)
     z = 2 * h + zl
-    xm, xp, x2 = (x + 3) % 4, (x + 1) % 4, (x + 2) % 4
-    ym, yp, y2 = (y + 3) % 4, (y + 1) % 4, (y + 2) % 4
+    xs = [x] + [lax.rem(x + d, 4) for d in range(1, 4)]
+    ys = [y] + [lax.rem(y + d, 4) for d in range(1, 4)]
+    zs = {d: lax.rem(z + d, 8) for d in (1, 2, 4, 6, 7)}
+    bases = {d: (lax.div(a, 2) * 4, lax.rem(a, 2) * 8) for d, a in zs.items()}
+    bases[0] = (h * 4, zl * 8)
+    _, xp, x2, xm = xs
+    _, yp, y2, ym = ys
 
     def at(dx=0, dy=0, dz=0, dc=0):
-        zz = (z + dz + 8) % 8
-        return (
-            (zz // 2) * 4 + (y + dy + 4) % 4,
-            (zz % 2) * 8 + ((x + dx + 4) % 4) * 2 + (c + dc) % 2,
-        )
+        wide_base, narrow_base = bases[dz % 8]
+        return wide_base + ys[dy % 4], narrow_base + 2 * xs[dx % 4] + (1 - c if dc else c)
 
     def send(src, dst, ss, rs, device):
         return pltpu.make_async_remote_copy(
@@ -199,7 +201,7 @@
         j = t // 2
         mid = (j % 3 + 1) // 2
         off = mid * (3 - 2 * (t % 2)) + (1 - mid) * (2 * (j // 3))
-        mm1((x + off) % 4, mid * (j - 1) + (1 - mid) * (t % 2))
+        mm1(lax.rem(x + off, 4), mid * (j - 1) + (1 - mid) * (t % 2))
         return carry
 
     lax.fori_loop(0, 8, step, 0)
@@ -252,7 +254,7 @@
             ycopy(n, 2, side).start()
 
     def zcopy(n, d):
-        return send(zb.at[n, (h + d) % 4], rz.at[n, d - 1], rz_ss.at[0], rz_rs.at[n], at(dz=2 * d))
+        return send(zb.at[n, lax.rem(h + d, 4)], rz.at[n, d - 1], rz_ss.at[0], rz_rs.at[n], at(dz=2 * d))
 
     def rs_c(n):
         wait(rym.at[n], ym_rs.at[n])
@@ -271,9 +273,10 @@
         return send(outv.at[n, y, h], outv.at[n, y, h], az_ss.at[0], az_rs.at[n], at(dz=2 * d))
 
     def aycopy(n, q):
-        side = q % 2
-        to, ss, rs = at(dy=1 - 2 * side), ay_ss.at[q // 2], ay_rs.at[n, q]
-        block = outv.at[n, y] if q < 2 else outv.at[n, (ym, yp)[side], :, :, cols(side)]
+        side, kind = q % 2, q // 2
+        to, ss, rs = at(dy=1 - 2 * side), ay_ss.at[kind], ay_rs.at[n, q]
+        part = cols(1 - side if kind == 2 else side)
+        block = outv.at[n, (ym, yp)[side] if kind == 1 else y, :, :, part]
         return send(block, block, ss, rs, to)
 
     def ag_f(n):
@@ -288,7 +291,7 @@
 
     def ag_g(n):
         wait(rz.at[n], az_rs.at[n])
-        for q in range(2):
+        for q in (0, 1, 4, 5):
             aycopy(n, q).start()
 
     def ag_h(n):
@@ -297,7 +300,7 @@
             aycopy(n, 2 + q).start()
 
     def ag_i(n):
-        for q in range(2, 4):
+        for q in range(2, 6):
             aycopy(n, q).wait_recv()
 
     def ccopy(n):
@@ -364,8 +367,8 @@
     wait(rym, ym_ss.at[0])
     wait(rz, rz_ss.at[0])
     wait(rz, az_ss.at[0])
-    wait(outv.at[pl.ds(0, 2)], ay_ss.at[0])
-    wait(outv.at[0], ay_ss.at[1])
+    for n in range(3):
+        wait(outv.at[0], ay_ss.at[n])
     wait(cnt_y, c_ss.at[0])
     wait(cnt_z, c_ss.at[1])
 
@@ -408,7 +411,7 @@
             dma((1,)), dma((NP, 2)), dma((1,)), dma((NP, 2)), dma((1,)), dma((4,)), dma((1,)), dma((8,)),
             dma((1,)), dma((4,)), dma((1,)), dma((4,)), dma((1,)), dma((4,)), pltpu.SemaphoreType.REGULAR,
             dma((1,)), dma((4, 2)), dma((1,)), dma((4,)), dma((1,)), dma((4,)),
-            dma((1,)), dma((4,)), dma((2,)), dma((4, 4)), dma((2,)), dma((2,)), dma((2,)),
+            dma((1,)), dma((4,)), dma((3,)), dma((4, 6)), dma((2,)), dma((2,)), dma((2,)),
         ],
         compiler_params=pltpu.CompilerParams(
             collective_id=0, has_side_effects=True, vmem_limit_bytes=51 << 20
@@ -416,7 +419,7 @@
         cost_estimate=pl.CostEstimate(
             flops=4 * 4096 * 1024 * D, bytes_accessed=4 << 20, transcendentals=4096 * 1024
         ),
-    )(points.reshape(2, 128, D), centroids)
+    )(*(pltpu.with_memory_space_constraint(a, pltpu.HBM) for a in (points.reshape(2, 128, D), centroids)))
     return out.reshape(1024, D), counts.reshape(1024)
 
 

time: 79.3 us -> 78 us (0.984)
  local copies, waits for them, and re-layouts: 2.73 us -> 1.74 us
    unnamed x4 -> x2, local copies, waits for them, and re-layouts: 2.73 us -> 1.74 us
where the time goes in v7:
time: 78 us; the launch traced here: 77.9 us
  Pallas kernels  75.6 us (97%)
  local copies, waits for them, and re-layouts  1.74 us (2%)
    pallas_call x1, Pallas kernels, on_device(): pl.pallas_call(kernel, out_shape=(jax.ShapeDtypeStruct((4, 4, 4, 16, D),...  75.6 us
    unnamed x2, local copies, waits for them, and re-layouts  1.74 us

profile of v7, /device:TPU:8, one launch (start us, length us, event | category | flops | bytes accessed | tf_op | source)
XLA Modules:
  0.0 77.9 jit_solution(3450036774277627829)
XLA Ops:
  0.6 75.6 %shard_map.41 = (bf16[4,4,4,16,768]{4,3,2,1,0:T(8,128)(2,1)S(1)}, f32[8,128]{1,0:T(8,128)S(1)}) custom-call(bf16[2,128,768]{2,1,0:T(8,128)(2,1)} %bitcast.5, bf16[1024,768]{1,0:T(8,128)(2,1)} %cen_in.1), custom_call_target="tpu_custom_call" | custom-call | flops 12884901888 | bytes 4194304 | tf_op jit(solution)/shard_map/pallas_call | solution.py:378
  76.2 1.1 %copy.6 = bf16[1024,768]{1,0:T(8,128)(2,1)} copy(bf16[1024,768]{1,0:T(8,128)(2,1)S(1)} %bitcast.3) | data formatting | bytes 3145728
  77.3 0.6 copy.7

commit v8 on v7

--- a/solution.py
+++ b/solution.py
@@ -98,10 +98,11 @@
     def ev1(p):
         for way in range(2):
             xcopy(p, way).wait_recv()
+        for k in (1, 2):
+            for way in range(2):
+                zpoints(p, way, k).start()
         for way in range(2):
             fcopy(p, way).start()
-            for k in (1, 2):
-                zpoints(p, way, k).start()
         for k in (1, 2):
             sib(k, p).start()
 
@@ -241,10 +242,12 @@
         return send(yb.at[n, near, :, part], rym.at[n, side, :, part], ym_ss.at[0], ym_rs.at[n], to)
 
     def rs_a(n):
-        yb[n] = acc[n].astype(BF16)
-        for kind in range(2):
-            for side in range(2):
-                ycopy(n, kind, side).start()
+        yb[n, y2] = acc[n, y2].astype(BF16)
+        for side in range(2):
+            ycopy(n, 0, side).start()
+        for side, near in ((0, yp), (1, ym)):
+            yb[n, near] = acc[n, near].astype(BF16)
+            ycopy(n, 1, side).start()
 
     def rs_b(n):
         for side, near in ((0, yp), (1, ym)):

time: 78 us -> 78.1 us (level)
  no operation moved by 1% of the time
where the time goes in v8:
time: 78.1 us; the launch traced here: 78 us
  Pallas kernels  75.6 us (97%)
  local copies, waits for them, and re-layouts  1.74 us (2%)
    pallas_call x1, Pallas kernels, on_device(): pl.pallas_call(kernel, out_shape=(jax.ShapeDtypeStruct((4, 4, 4, 16, D),...  75.6 us
    unnamed x2, local copies, waits for them, and re-layouts  1.74 us

profile of v8, /device:TPU:8, one launch (start us, length us, event | category | flops | bytes accessed | tf_op | source)
XLA Modules:
  0.0 78.0 jit_solution(1876283141828588684)
XLA Ops:
  0.6 75.6 %shard_map.41 = (bf16[4,4,4,16,768]{4,3,2,1,0:T(8,128)(2,1)S(1)}, f32[8,128]{1,0:T(8,128)S(1)}) custom-call(bf16[2,128,768]{2,1,0:T(8,128)(2,1)} %bitcast.5, bf16[1024,768]{1,0:T(8,128)(2,1)} %cen_in.1), custom_call_target="tpu_custom_call" | custom-call | flops 12884901888 | bytes 4194304 | tf_op jit(solution)/shard_map/pallas_call | solution.py:381
  76.2 1.1 %copy.6 = bf16[1024,768]{1,0:T(8,128)(2,1)} copy(bf16[1024,768]{1,0:T(8,128)(2,1)S(1)} %bitcast.3) | data formatting | bytes 3145728
  77.4 0.6 copy.7

commit v9 on v7

--- a/solution.py
+++ b/solution.py
@@ -347,11 +347,11 @@
         chunk(2, rs_c)
         chunk(5, ag_g)
         pl.when(s == 6)(cnt_a)
-        chunk(6, ag_h)
+        chunk(7, ag_h)
         pl.when(s == 7)(cnt_b)
         return carry
 
-    lax.fori_loop(0, 10, wave, 0)
+    lax.fori_loop(0, 11, wave, 0)
     cnt_c()
     for n in range(4):
         ag_i(n)

time: 78 us -> 78.1 us (level)
  no operation moved by 1% of the time
where the time goes in v9:
time: 78.1 us; the launch traced here: 77.9 us
  Pallas kernels  75.6 us (97%)
  local copies, waits for them, and re-layouts  1.74 us (2%)
    pallas_call x1, Pallas kernels, on_device(): pl.pallas_call(kernel, out_shape=(jax.ShapeDtypeStruct((4, 4, 4, 16, D),...  75.6 us
    unnamed x2, local copies, waits for them, and re-layouts  1.74 us

profile of v9, /device:TPU:8, one launch (start us, length us, event | category | flops | bytes accessed | tf_op | source)
XLA Modules:
  0.0 77.9 jit_solution(6937307517457047334)
XLA Ops:
  0.6 75.6 %shard_map.41 = (bf16[4,4,4,16,768]{4,3,2,1,0:T(8,128)(2,1)S(1)}, f32[8,128]{1,0:T(8,128)S(1)}) custom-call(bf16[2,128,768]{2,1,0:T(8,128)(2,1)} %bitcast.5, bf16[1024,768]{1,0:T(8,128)(2,1)} %cen_in.1), custom_call_target="tpu_custom_call" | custom-call | flops 12884901888 | bytes 4194304 | tf_op jit(solution)/shard_map/pallas_call | solution.py:378
  76.2 1.1 %copy.6 = bf16[1024,768]{1,0:T(8,128)(2,1)} copy(bf16[1024,768]{1,0:T(8,128)(2,1)S(1)} %bitcast.3) | data formatting | bytes 3145728
  77.3 0.6 copy.7
